TPU v7x, 128 devices: a whole 4x4x4 slice. The times are simulated.
128 devices in a mesh: wide: 32 (over x, z, core), narrow: 4 (over y).
Axes of the slice: x: 4, y: 4, z: 4, core: 2. Of those that a mesh axis runs over, the one named last changes fastest.
Arguments:
- water_depth: float32 [8, 8, 163840], P(None, None, ('wide', 'narrow')), may hold values from 2 to 3
- momentum: float32 [2, 8, 8, 163840], P(None, None, None, ('wide', 'narrow')), may hold values from -3 to 3
- bathymetry: float32 [8, 8, 163840], P(None, None, ('wide', 'narrow')), may hold values from -0.5 to 0.5
- levels: int32 [163840], P(('wide', 'narrow')), may hold values from 0 to 1, as said below
- face_kind: int32 [4, 163840], P(None, ('wide', 'narrow')), may hold values from 0 to 3, as said below
- send_face: int32 [18432], P(('wide', 'narrow')), may hold values from 0 to 5119, as said below
- trace_src: int32 [4, 163840], P(None, ('wide', 'narrow')), may hold values from 0 to 5263, as said below
- return_face: int32 [12288], P(('wide', 'narrow')), may hold values from 0 to 5119, as said below
- mortar_src: int32 [2, 4, 163840], P(None, None, ('wide', 'narrow')), may hold values from 0 to 5215, as said below
Outputs:
- new_depth: float32 [8, 8, 163840], P(None, None, ('wide', 'narrow'))
- new_momentum: float32 [2, 8, 8, 163840], P(None, None, None, ('wide', 'narrow'))
Inputs may be any that keep to these rules, and one draw needn't show every extreme that they name: `levels`: the mesh is a periodic forest of 32 x 8 trees of 16 x 16 blocks; the device at wide index w and narrow index n holds trees (w, 2n) and (w, 2n + 1) in that order; a block is one element of level 0 or four of level 1; elements of a tree in Morton order of blocks, children in Morton order. `face_kind`: 0: conforming neighbour; 1 or 2: a level 1 face whose neighbour is a level 0 face, touching its lower or upper half; 3: a level 0 face met by two level 1 faces. `send_face`: Every block is full on some device in every draw. `trace_src`: for faces of kinds 0 to 2; 0 on faces of kind 3. `return_face`: Every block is full on some device in every draw. `mortar_src`: lower and upper half for faces of kind 3, into [projected, returned]; 0 elsewhere.
All inputs are finite; a program needn't handle non-finite values.
Results may differ from a plain program's by a relative error of at most 0.0003.
Values sent between devices are 32-bit elements; how exact they have to be, the bound alone decides.
No kernel may reach another device: no remote copies, remote signals or barrier semaphores. Data moves between devices by JAX's collectives and lax.ppermute only.
A program may use at most 64 MiB of HBM per device.

v0:
```python
import jax
import jax.numpy as jnp
import numpy as np
from jax import lax
from jax.sharding import PartitionSpec as P

CAP_X = 48
CAP_Y = 24
RET_X = 32
RET_Y = 16


gravity = 1.0
time_step = 0.005


def from_behind(block, axis, distance):
    devices = range(lax.axis_size(axis))
    route = [((i - distance) % len(devices), i) for i in devices]
    return lax.ppermute(block, axis, route)


def legendre_pair(points, degree):
    before = np.ones(points.shape)
    current = points * 1.0
    for order in range(2, degree + 1):
        following = ((2.0 * order - 1.0) * points * current - (order - 1.0) * before) / order
        before = current
        current = following
    return (current, before)


def lgl_tables():
    degree = 7
    point_count = degree + 1
    points = -np.cos(np.pi * np.arange(point_count) / degree)
    for sweep in range(100):
        top_value, below_value = legendre_pair(points, degree)
        points = points - (points * top_value - below_value) / (point_count * top_value)
    points[0] = -1.0
    points[-1] = 1.0
    values = legendre_pair(points, degree)[0]
    weights = 2.0 / (degree * point_count * values * values)
    derivative = np.zeros((point_count, point_count))
    for row_id in range(point_count):
        for col_id in range(point_count):
            if row_id != col_id:
                derivative[row_id, col_id] = values[row_id] / (
                    values[col_id] * (points[row_id] - points[col_id])
                )
    derivative[0, 0] = -degree * point_count / 4.0
    derivative[-1, -1] = degree * point_count / 4.0

    def lagrange(targets):
        lagrange_table = np.ones((point_count, point_count))
        for col_id in range(point_count):
            for other_id in range(point_count):
                if other_id != col_id:
                    lagrange_table[:, col_id] = (
                        lagrange_table[:, col_id]
                        * (targets - points[other_id])
                        / (points[col_id] - points[other_id])
                    )
        return lagrange_table

    interp_lower = lagrange((points - 1.0) / 2.0)
    interp_upper = lagrange((points + 1.0) / 2.0)
    proj_lower = 0.5 * interp_lower.T * weights[None, :] / weights[:, None]
    proj_upper = 0.5 * interp_upper.T * weights[None, :] / weights[:, None]
    lift_end = 1.0 / weights[0]
    return (
        lift_end,
        jnp.asarray(derivative, jnp.float32),
        jnp.asarray(interp_lower, jnp.float32),
        jnp.asarray(interp_upper, jnp.float32),
        jnp.asarray(proj_lower, jnp.float32),
        jnp.asarray(proj_upper, jnp.float32),
    )


def point_pair(height_l, normal_l, tangent_l, height_r, normal_r, tangent_r):
    mean_h = 0.5 * (height_l + height_r)
    mean_n = 0.5 * (normal_l + normal_r)
    mean_t = 0.5 * (tangent_l + tangent_r)
    square_h = 0.5 * (height_l * height_l + height_r * height_r)
    return (
        mean_h * mean_n,
        mean_h * mean_n * mean_n + 0.5 * gravity * square_h,
        mean_h * mean_n * mean_t,
    )


def face_traces(height, mom_x, mom_y, bed):
    stacked = jnp.stack([height, mom_x, mom_y, bed])
    sides = jnp.stack([stacked[:, 0], stacked[:, -1], stacked[:, :, 0], stacked[:, :, -1]], axis=2)
    return sides.reshape(32, -1)


def face_flux(own, other, face_id):
    normal_sign = -1.0 if face_id % 2 == 0 else 1.0
    normal_id = 1 if face_id < 2 else 2
    tangent_id = 3 - normal_id
    vel_n_own = own[normal_id] / own[0]
    vel_t_own = own[tangent_id] / own[0]
    vel_n_other = other[normal_id] / other[0]
    vel_t_other = other[tangent_id] / other[0]
    flux_mass, flux_normal, flux_tangent = point_pair(
        own[0], vel_n_own, vel_t_own, other[0], vel_n_other, vel_t_other
    )
    speed = jnp.maximum(
        jnp.abs(vel_n_own) + jnp.sqrt(gravity * own[0]),
        jnp.abs(vel_n_other) + jnp.sqrt(gravity * other[0]),
    )
    num_h = normal_sign * flux_mass - 0.5 * speed * (other[0] + other[3] - (own[0] + own[3]))
    num_n = normal_sign * flux_normal - 0.5 * speed * (other[normal_id] - own[normal_id])
    num_t = normal_sign * flux_tangent - 0.5 * speed * (other[tangent_id] - own[tangent_id])
    phys_h = normal_sign * own[normal_id]
    phys_n = normal_sign * (own[normal_id] * vel_n_own + 0.5 * gravity * own[0] * own[0])
    phys_t = normal_sign * own[normal_id] * vel_t_own
    if normal_id == 1:
        return (jnp.stack([num_h, num_n, num_t]), jnp.stack([phys_h, phys_n, phys_t]))
    return (jnp.stack([num_h, num_t, num_n]), jnp.stack([phys_h, phys_t, phys_n]))


def surface_fluxes(local, received, kinds, trace_index, tables):
    element_count = kinds.shape[1]
    interp_lower, interp_upper, proj_lower, proj_upper = (
        tables[2],
        tables[3],
        tables[4],
        tables[5],
    )
    highest = lax.Precision.HIGHEST
    trace_pool = jnp.concatenate([local, received], axis=1)
    gathered = trace_pool[:, trace_index.reshape(-1)].reshape(4, 8, 4, element_count)
    own_all = local.reshape(4, 8, 4, element_count)
    from_lower = jnp.einsum("ab,cbfe->cafe", interp_lower, gathered, precision=highest)
    from_upper = jnp.einsum("ab,cbfe->cafe", interp_upper, gathered, precision=highest)
    selector = kinds[None, None]
    other_all = jnp.where(selector == 1, from_lower, jnp.where(selector == 2, from_upper, gathered))
    numeric_list = []
    physical_list = []
    for face_id in range(4):
        numeric_face, physical_face = face_flux(
            own_all[:, :, face_id], other_all[:, :, face_id], face_id
        )
        numeric_list.append(numeric_face)
        physical_list.append(physical_face)
    numeric = jnp.stack(numeric_list, axis=2)
    physical = jnp.stack(physical_list, axis=2)
    onto_lower = jnp.einsum("ab,cbfe->cafe", proj_lower, numeric, precision=highest)
    onto_upper = jnp.einsum("ab,cbfe->cafe", proj_upper, numeric, precision=highest)
    projected = jnp.where(selector == 1, onto_lower, onto_upper)
    return (numeric, physical, projected.reshape(24, -1))


def volume_rates(height, mom_x, mom_y, bed, derivative):
    highest = lax.Precision.HIGHEST
    vel_x = mom_x / height
    vel_y = mom_y / height
    pair_x = point_pair(
        height[:, None], vel_x[:, None], vel_y[:, None], height[None], vel_x[None], vel_y[None]
    )
    factor_x = 2.0 * derivative[:, :, None, None]
    rate_h = -jnp.sum(factor_x * pair_x[0], axis=1)
    rate_x = -jnp.sum(factor_x * pair_x[1], axis=1)
    rate_y = -jnp.sum(factor_x * pair_x[2], axis=1)
    pair_y = point_pair(
        height[:, :, None],
        vel_y[:, :, None],
        vel_x[:, :, None],
        height[:, None],
        vel_y[:, None],
        vel_x[:, None],
    )
    factor_y = 2.0 * derivative[None, :, :, None]
    rate_h = rate_h - jnp.sum(factor_y * pair_y[0], axis=2)
    rate_y = rate_y - jnp.sum(factor_y * pair_y[1], axis=2)
    rate_x = rate_x - jnp.sum(factor_y * pair_y[2], axis=2)
    slope_x = jnp.einsum("ik,kje->ije", derivative, bed, precision=highest)
    slope_y = jnp.einsum("jk,ike->ije", derivative, bed, precision=highest)
    rate_x = rate_x - gravity * height * slope_x
    rate_y = rate_y - gravity * height * slope_y
    return jnp.stack([rate_h, rate_x, rate_y])


def mortar_from_pool(pool_two, mortar_index, element_count):
    return (
        pool_two[:, mortar_index[0].reshape(-1)] + pool_two[:, mortar_index[1].reshape(-1)]
    ).reshape(3, 8, 4, element_count)


def finish_section(height, momentum, bed, levels, numeric, physical, kinds, mortar, tables):
    lift_end, derivative = (tables[0], tables[1])
    numeric = jnp.where(kinds[None, None] == 3, -mortar, numeric)
    flux_jump = numeric - physical
    metric = (1 + levels).astype(jnp.float32)
    rate_all = volume_rates(height, momentum[0], momentum[1], bed, derivative) * metric
    lifted = lift_end * metric * flux_jump
    rate_all = rate_all.at[:, 0].add(-lifted[:, :, 0])
    rate_all = rate_all.at[:, -1].add(-lifted[:, :, 1])
    rate_all = rate_all.at[:, :, 0].add(-lifted[:, :, 2])
    rate_all = rate_all.at[:, :, -1].add(-lifted[:, :, 3])
    new_height = height + time_step * rate_all[0]
    new_moment = momentum + time_step * rate_all[1:]
    return (new_height, new_moment)


def split_four(buffer, cap_x, cap_y):
    return (
        buffer[:, :cap_x],
        buffer[:, cap_x : 2 * cap_x],
        buffer[:, 2 * cap_x : 2 * cap_x + cap_y],
        buffer[:, 2 * cap_x + cap_y :],
    )


def on_device(
    water_depth,
    momentum,
    bathymetry,
    levels,
    face_kind,
    send_face,
    trace_src,
    return_face,
    mortar_src,
):
    tables = lgl_tables()
    element_count = face_kind.shape[1]
    local = face_traces(water_depth, momentum[0], momentum[1], bathymetry)
    wide_down, wide_up, narrow_down, narrow_up = split_four(local[:, send_face], CAP_X, CAP_Y)
    wide_parts = []
    for trace_part, shift_by in ((wide_up, 1), (wide_down, -1)):
        wide_parts.append(from_behind(trace_part, "wide", shift_by))
    narrow_parts = []
    for trace_part, shift_by in ((narrow_up, 1), (narrow_down, -1)):
        narrow_parts.append(from_behind(trace_part, "narrow", shift_by))
    received = jnp.concatenate(wide_parts + narrow_parts, axis=1)
    numeric, physical, projected = surface_fluxes(local, received, face_kind, trace_src, tables)
    back_wd, back_wu, back_nd, back_nu = split_four(projected[:, return_face], RET_X, RET_Y)
    wide_back = []
    for flux_part, shift_by in ((back_wu, 1), (back_wd, -1)):
        wide_back.append(from_behind(flux_part, "wide", shift_by))
    narrow_back = []
    for flux_part, shift_by in ((back_nu, 1), (back_nd, -1)):
        narrow_back.append(from_behind(flux_part, "narrow", shift_by))
    returned = jnp.concatenate(wide_back + narrow_back, axis=1)
    pool_two = jnp.concatenate([projected, returned], axis=1)
    mortar = mortar_from_pool(pool_two, mortar_src, element_count)
    return finish_section(
        water_depth, momentum, bathymetry, levels, numeric, physical, face_kind, mortar, tables
    )


def solution(mesh):
    placed = (
        P(None, None, ("wide", "narrow")),
        P(None, None, None, ("wide", "narrow")),
        P(None, None, ("wide", "narrow")),
        P(("wide", "narrow")),
        P(None, ("wide", "narrow")),
        P(("wide", "narrow")),
        P(None, ("wide", "narrow")),
        P(("wide", "narrow")),
        P(None, None, ("wide", "narrow")),
    )
    return jax.shard_map(
        on_device,
        mesh=mesh,
        in_specs=placed,
        out_specs=(P(None, None, ("wide", "narrow")), P(None, None, None, ("wide", "narrow"))),
        check_vma=False,
    )
```

profile of v0, /device:TPU:0, one launch (start us, length us, event | category | flops | bytes accessed | tf_op | source)
XLA Modules:
  0.0 140.0 jit_solution(13409769899647583447)
XLA Ops:
  0.7 1.1 copy.406
  1.8 1.5 %fusion.89 = f32[8,8,1280]{2,0,1:T(8,128)S(1)} fusion(f32[8,8,1]{1,0,2:T(8,128)} %constant.163, f32[8,8,1280]{2,1,0:T(8,128)} %param.24), kind=kOutput, calls=%fused_computation.222 | convolution fusion | flops 7864320 | bytes 655616 | tf_op jit(solution)/shard_map/jk,ike->ije/dot_general | solution.py:181
  3.3 1.2 bitcast_divide_fusion
  4.6 6.4 %multiply_reduce_fusion.2 = (f32[8,8,1280]{2,1,0:T(8,128)}, f32[8,8,1280]{2,1,0:T(8,128)S(1)}, f32[8,8,1280]{2,1,0:T(8,128)S(1)}, f32[8,8,1280]{2,1,0:T(8,128)S(...) fusion(f32[8,8,1280]{2,1,0:T(8,128)S(1)} %get-tuple-element.89, f32[8,8,1280]{2,1,0:T(8,128)S(1)} %get-tuple-element.88, ...), kind=kLoop, calls=%fused_computation.8 | loop fusion | flops 23101440 | bytes 3277056 | tf_op jit(solution)/shard_map/reduce_sum | solution.py:179
  10.9 1.4 %copy_bitcast_fusion.1 = (f32[1,8,8,1280]{3,1,2,0:T(8,128)S(1)}, f32[1,8,8,1280]{3,1,2,0:T(8,128)}, f32[1,8,8,1280]{3,1,2,0:T(8,128)}) fusion(f32[8,8,1280]{2,1,0:T(8,128)S(1)} %copy-done, f32[8,8,1280]{2,0,1:T(8,128)S(1)} %fusion.89, f32[8,8,1280]{2,1,0:T(8,128)S(1)} %get-tuple-element.61, f32[8,8,1280]{2,1,0:T(8,128)S(1)} %get-tuple-element.59, ...), kind=kLoop, calls=%fused_computation.53 | loop fusion | flops 491520 | bytes 2949120 | tf_op jit(solution)/shard_map/broadcast_in_dim | solution.py:162
  12.5 0.9 fusion.84
  14.6 1.0 copy.270
  15.6 1.8 %copy.208 = f32[32,5120]{0,1:T(8,128)S(1)} copy(f32[32,5120]{1,0:T(8,128)} %bitcast.553) | data formatting | bytes 1310720 | tf_op jit(solution)/shard_map/reshape | solution.py:96
  18.1 0.7 gather_fusion
  18.9 5.8 %collective-permute-start.1 = (f32[32,48]{0,1:T(8,128)S(1)}, f32[32,48]{0,1:T(8,128)S(1)}, u32[]{:S(2)}, u32[]{:S(2)}) collective-permute-start(f32[32,48]{0,1:T(8,128)S(1)} %get-tuple-element.109), channel_id=1, source_target_pairs={{4,0},{8,4},{12,8},{16,12},{20,16},{24,20},{28,24},{32,28},{36,32}... | collective-permute-start | bytes 18440 | tf_op jit(solution)/shard_map/ppermute | solution.py:20
  24.7 1.6 %collective-permute-start.2 = (f32[32,24]{0,1:T(8,128)S(1)}, f32[32,24]{0,1:T(8,128)S(1)}, u32[]{:S(2)}, u32[]{:S(2)}) collective-permute-start(f32[32,24]{0,1:T(8,128)S(1)} %get-tuple-element.108), channel_id=1, source_target_pairs={{3,0},{0,1},{1,2},{2,3},{7,4},{4,5},{5,6},{6,7},{11,8},{8,9},{9,10... | collective-permute-start | bytes 9224 | tf_op jit(solution)/shard_map/ppermute | solution.py:20
  26.4 1.9 %collective-permute-start.3 = (f32[32,24]{0,1:T(8,128)S(1)}, f32[32,24]{0,1:T(8,128)S(1)}, u32[]{:S(2)}, u32[]{:S(2)}) collective-permute-start(f32[32,24]{0,1:T(8,128)S(1)} %get-tuple-element.107), channel_id=1, source_target_pairs={{1,0},{2,1},{3,2},{0,3},{5,4},{6,5},{7,6},{4,7},{9,8},{10,9},{11,1... | collective-permute-start | bytes 9224 | tf_op jit(solution)/shard_map/ppermute | solution.py:20
  28.3 1.9 %constant_dynamic-update-slice_fusion.6 = f32[32,5264]{0,1:T(8,128)S(1)} fusion(f32[32,5120]{0,1:T(8,128)} %copy-done.4), kind=kLoop, calls=%fused_computation.185 | loop fusion | bytes 3276800
  30.4 0.7 slice_bitcast_fusion.5
  31.2 0.7 fusion.82
  32.7 0.7 fusion.5
  34.8 0.7 slice.493
  35.6 17.8 %gather_fusion.1 = f32[5120,32]{1,0:T(8,128)} fusion(f32[32,5264]{0,1:T(8,128)S(1)} %constant_dynamic-update-slice_fusion.2, s32[5120]{0:T(1024)S(1)} %broadcast_clamp_fusion.2), kind=kCustom, calls=%fused_computation.1 | custom fusion | bytes 1331200 | tf_op jit(solution)/shard_map/gather | solution.py:135
  53.4 2.1 %copy.209 = f32[32,5120]{1,0:T(8,128)S(1)} copy(f32[32,5120]{0,1:T(8,128)} %bitcast.552) | data formatting | bytes 1310720 | tf_op jit(solution)/shard_map/gather | solution.py:135
  55.6 0.7 convolution_bitcast_fusion.1
  56.3 0.7 fusion.3
  57.0 1.0 fusion.38
  58.0 1.6 %multiply_subtract_fusion.3 = (f32[1,8,1280]{2,1,0:T(8,128)S(1)}, f32[1,8,1280]{2,1,0:T(8,128)S(1)}, f32[1,8,1280]{2,1,0:T(8,128)S(1)}, f32[1,8,1280]{2,1,0:T(8,...) fusion(f32[4,8,4,1280]{3,1,2,0:T(8,128)S(1)} %fusion.3, f32[1,8,1280]{2,1,0:T(8,128)S(1)} %get-tuple-element.72, ...), kind=kLoop, calls=%fused_computation.159 | loop fusion | flops 645120 | bytes 696320 | tf_op jit(solution)/shard_map/sub | solution.py:116
  59.6 1.4 multiply_subtract_fusion.6
  61.7 0.9 fusion.43
  62.6 0.9 fusion.57
  64.7 2.2 %copy.237 = f32[24,5120]{0,1:T(8,128)} copy(f32[24,5120]{1,0:T(8,128)S(1)} %bitcast.554) | data formatting | bytes 983040 | tf_op jit(solution)/shard_map/reshape | solution.py:154
  67.0 2.0 %constant_dynamic-update-slice_fusion.11 = f32[24,5216]{0,1:T(8,128)S(1)} fusion(f32[24,5120]{0,1:T(8,128)} %copy.237), kind=kLoop, calls=%fused_computation.190 | loop fusion | bytes 3112960
  69.0 3.1 %gather_fusion.2 = f32[96,24]{1,0:T(8,128)} fusion(f32[24,5120]{0,1:T(8,128)} %copy.237, s32[1024]{0:T(1024)} %get-tuple-element.125), kind=kCustom, calls=%fused_computation.2 | custom fusion | bytes 18816 | tf_op jit(solution)/shard_map/gather | solution.py:241
  72.0 0.7 fusion.88
  72.8 0.7 maximum_bitcast_fusion.8
  73.5 0.7 maximum_bitcast_fusion.7
  74.1 0.7 maximum_bitcast_fusion.6
  74.9 0.7 fusion.87
  75.6 0.7 copy.243
  76.3 5.1 %collective-permute-start.5 = (f32[24,32]{0,1:T(8,128)S(1)}, f32[24,32]{0,1:T(8,128)S(1)}, u32[]{:S(2)}, u32[]{:S(2)}) collective-permute-start(f32[24,32]{0,1:T(8,128)S(1)} %get-tuple-element.113), channel_id=1, source_target_pairs={{4,0},{8,4},{12,8},{16,12},{20,16},{24,20},{28,24},{32,28},{36,32}... | collective-permute-start | bytes 9224 | tf_op jit(solution)/shard_map/ppermute | solution.py:20
  81.7 2.9 %collective-permute-start.7 = (f32[24,16]{0,1:T(8,128)S(1)}, f32[24,16]{0,1:T(8,128)S(1)}, u32[]{:S(2)}, u32[]{:S(2)}) collective-permute-start(f32[24,16]{0,1:T(8,128)S(1)} %get-tuple-element.111), channel_id=1, source_target_pairs={{1,0},{2,1},{3,2},{0,3},{5,4},{6,5},{7,6},{4,7},{9,8},{10,9},{11,1... | collective-permute-start | bytes 4616 | tf_op jit(solution)/shard_map/ppermute | solution.py:20
  84.6 1.6 %collective-permute-done.6 = f32[24,16]{0,1:T(8,128)S(1)} collective-permute-done((f32[24,16]{0,1:T(8,128)S(1)}, f32[24,16]{0,1:T(8,128)S(1)}, u32[]{:S(2)}, u32[]{:S(2)}) %collective-permute-start.6) | collective-permute-done | bytes 1568 | tf_op jit(solution)/shard_map/ppermute | solution.py:20
  86.2 17.8 %gather_fusion.3 = f32[5120,24]{1,0:T(8,128)} fusion(f32[24,5216]{0,1:T(8,128)S(1)} %constant_dynamic-update-slice_fusion.7, s32[5120]{0:T(1024)S(1)} %copy-done.25), kind=kCustom, calls=%fused_computation.3 | custom fusion | bytes 1003520 | tf_op jit(solution)/shard_map/gather | solution.py:189
  104.0 17.7 %gather_fusion.4 = f32[5120,24]{1,0:T(8,128)} fusion(f32[24,5216]{0,1:T(8,128)S(1)} %constant_dynamic-update-slice_fusion.7, s32[5120]{0:T(1024)S(1)} %copy-done.24), kind=kCustom, calls=%fused_computation.4 | custom fusion | bytes 1003520 | tf_op jit(solution)/shard_map/gather | solution.py:189
  121.7 2.8 %negate_bitcast_fusion = f32[24,5120]{0,1:T(8,128)S(1)} fusion(f32[5120,24]{1,0:T(8,128)} %gather_fusion.3, f32[5120,24]{1,0:T(8,128)} %gather_fusion.4), kind=kLoop, calls=%fused_computation.5 | loop fusion | flops 245760 | bytes 1474560 | tf_op jit(solution)/shard_map/neg | solution.py:195
  124.6 0.7 copy.238
  125.6 1.5 %fusion.7 = f32[3,8,4,1280]{3,1,2,0:T(8,128)S(1)} fusion(f32[3,8,1,1280]{3,1,2,0:T(8,128)} %maximum_bitcast_fusion.8, f32[3,8,1,1280]{3,1,2,0:T(8,128)} %maximum_bitcast_fusion.7, f32[3,8,1,1280]{3,1,2,0:T(8,128)} %maximum_bitcast_fusion.6, f32[3,8,1,1280]{3,1,2,0:T(8,128)} %copy.243, f32[1280]{0:T(1024)S(1)} %copy-done.28, f32[3,8,4,1280]{3,2,1,0:T(4,128)S(1)} %neg.57, ...), kind=kLoop, calls=%fused_computation.30 | loop fusion | flops 1105920 | bytes 1976320 | tf_op jit(solution)/shard_map/mul | solution.py:199
  127.0 0.9 fusion.24
  128.1 4.6 %scatter-add.14 = f32[3,8,8,1280]{3,1,2,0:T(8,128)S(1)} dynamic-update-slice(f32[3,8,8,1280]{3,1,2,0:T(8,128)S(1)} %copy-done.6, f32[3,1,8,1280]{3,1,2,0:T(1,128)S(1)} %copy.247, s32[]{:T(128)} %constant.147.clone.1, s32[]{:T(128)} %constant.147.clone.1, s32[]{:T(128)} %constant.147.clone.1, s32[]{:T(128)} %constant.147.clone.1) | dynamic-update-slice | bytes 245764 | tf_op jit(solution)/shard_map/scatter-add | solution.py:200
  133.0 4.6 %scatter-add.15 = f32[3,8,8,1280]{3,1,2,0:T(8,128)S(1)} dynamic-update-slice(f32[3,8,8,1280]{3,1,2,0:T(8,128)S(1)} %scatter-add.14, f32[3,1,8,1280]{3,1,2,0:T(1,128)S(1)} %copy.249, s32[]{:T(128)} %constant.147.clone.1, s32[]{:T(128)} %constant.153.clone.1, s32[]{:T(128)} %constant.147.clone.1, s32[]{:T(128)} %constant.147.clone.1) | dynamic-update-slice | bytes 245764 | tf_op jit(solution)/shard_map/scatter-add | solution.py:201
  138.1 0.8 copy.252
  138.9 1.0 copy.253
  (150 shorter events, 8.2 us)
Async XLA Ops:
  0.6 3.9 %copy-start.35 = (f32[8,8]{1,0:T(8,128)S(1)}, f32[8,8]{1,0:T(8,128)}, u32[]{:S(2)}) copy-start(f32[8,8]{1,0:T(8,128)} %constant.162) | copy-start | bytes 772
  0.6 3.9 %copy-start = (f32[8,8,1280]{2,1,0:T(8,128)S(1)}, f32[8,8,1280]{2,1,0:T(8,128)}, u32[]{:S(2)}) copy-start(f32[8,8,1280]{2,1,0:T(8,128)} %param.22) | copy-start | bytes 983044
  1.8 10.8 %copy-start.13 = (f32[8,8,1280]{2,0,1:T(8,128)}, f32[8,8,1280]{2,0,1:T(8,128)S(1)}, u32[]{:S(2)}) copy-start(f32[8,8,1280]{2,0,1:T(8,128)S(1)} %copy.406) | copy-start | bytes 983044
  10.9 1.5 %copy-start.1 = (f32[2,8,8,1280]{3,2,1,0:T(8,128)S(1)}, f32[2,8,8,1280]{3,2,1,0:T(8,128)}, u32[]{:S(2)}) copy-start(f32[2,8,8,1280]{3,2,1,0:T(8,128)} %param.23) | copy-start | bytes 1966084
  14.6 2.8 %copy-start.41 = (s32[96]{0:T(128)S(1)}, s32[96]{0:T(128)}, u32[]{:S(2)}) copy-start(s32[96]{0:T(128)} %param.29) | copy-start | bytes 1156
  14.6 2.8 %copy-start.40 = (s32[144]{0:T(256)S(1)}, s32[144]{0:T(256)}, u32[]{:S(2)}) copy-start(s32[144]{0:T(256)} %param.27) | copy-start | bytes 1732
  17.4 8.9 %copy-start.4 = (f32[32,5120]{0,1:T(8,128)}, f32[32,5120]{0,1:T(8,128)S(1)}, u32[]{:S(2)}) copy-start(f32[32,5120]{0,1:T(8,128)S(1)} %copy.208) | copy-start | bytes 1966084
  18.8 16.8 %collective-permute-start = (f32[32,48]{0,1:T(8,128)S(1)}, f32[32,48]{0,1:T(8,128)S(1)}, u32[]{:S(2)}, u32[]{:S(2)}) collective-permute-start(f32[32,48]{0,1:T(8,128)S(1)} %get-tuple-element.110), channel_id=1, source_target_pairs={{124,0},{0,4},{4,8},{8,12},{12,16},{16,20},{20,24},{24,28},{28,32}... | collective-permute-start | bytes 18440 | tf_op jit(solution)/shard_map/ppermute | solution.py:20
  18.9 16.7 %collective-permute-start.1 = (f32[32,48]{0,1:T(8,128)S(1)}, f32[32,48]{0,1:T(8,128)S(1)}, u32[]{:S(2)}, u32[]{:S(2)}) collective-permute-start(f32[32,48]{0,1:T(8,128)S(1)} %get-tuple-element.109), channel_id=1, source_target_pairs={{4,0},{8,4},{12,8},{16,12},{20,16},{24,20},{28,24},{32,28},{36,32}... | collective-permute-start | bytes 18440 | tf_op jit(solution)/shard_map/ppermute | solution.py:20
  24.7 10.9 %collective-permute-start.2 = (f32[32,24]{0,1:T(8,128)S(1)}, f32[32,24]{0,1:T(8,128)S(1)}, u32[]{:S(2)}, u32[]{:S(2)}) collective-permute-start(f32[32,24]{0,1:T(8,128)S(1)} %get-tuple-element.108), channel_id=1, source_target_pairs={{3,0},{0,1},{1,2},{2,3},{7,4},{4,5},{5,6},{6,7},{11,8},{8,9},{9,10... | collective-permute-start | bytes 9224 | tf_op jit(solution)/shard_map/ppermute | solution.py:20
  26.3 3.9 %copy-start.2 = (f32[2,8,8,1280]{3,2,1,0:T(8,128)S(1)}, f32[2,8,8,1280]{3,2,1,0:T(8,128)}, u32[]{:S(2)}) copy-start(f32[2,8,8,1280]{3,2,1,0:T(8,128)} %param.23) | copy-start | bytes 1966084
  26.3 5.6 %copy-start.29 = (s32[1280]{0:T(1024)S(1)}, s32[1280]{0:T(1024)}, u32[]{:S(2)}) copy-start(s32[1280]{0:T(1024)} %param.25) | copy-start | bytes 15364
  26.3 5.6 %copy-start.32 = (s32[4,1280]{1,0:T(4,128)S(1)}, s32[4,1280]{1,0:T(4,128)}, u32[]{:S(2)}) copy-start(s32[4,1280]{1,0:T(4,128)} %param.28) | copy-start | bytes 61444
  26.3 5.6 %copy-start.33 = (s32[4,1280]{1,0:T(4,128)S(1)}, s32[4,1280]{1,0:T(4,128)}, u32[]{:S(2)}) copy-start(s32[4,1280]{1,0:T(4,128)} %param.26) | copy-start | bytes 61444
  26.3 6.2 %copy-start.27 = (s32[2,4,1280]{2,1,0:T(4,128)S(1)}, s32[2,4,1280]{2,1,0:T(4,128)}, u32[]{:S(2)}) copy-start(s32[2,4,1280]{2,1,0:T(4,128)} %param.30) | copy-start | bytes 122884
  26.3 6.4 %copy-start.7 = (f32[8,8,1280]{2,1,0:T(8,128)S(1)}, f32[8,8,1280]{2,1,0:T(8,128)}, u32[]{:S(2)}) copy-start(f32[8,8,1280]{2,1,0:T(8,128)} %param.24) | copy-start | bytes 983044
  26.3 6.4 %copy-start.14 = (f32[8,8,1280]{2,1,0:T(8,128)S(1)}, f32[8,8,1280]{2,1,0:T(8,128)}, u32[]{:S(2)}) copy-start(f32[8,8,1280]{2,1,0:T(8,128)} %get-tuple-element.58) | copy-start | bytes 983044
  26.3 6.4 %copy-start.15 = (f32[8,8,1280]{2,1,0:T(8,128)S(1)}, f32[8,8,1280]{2,1,0:T(8,128)}, u32[]{:S(2)}) copy-start(f32[8,8,1280]{2,1,0:T(8,128)} %get-tuple-element.62) | copy-start | bytes 983044
  26.3 6.4 %copy-start.34 = (f32[8,8,1]{1,0,2:T(8,128)S(1)}, f32[8,8,1]{1,0,2:T(8,128)}, u32[]{:S(2)}) copy-start(f32[8,8,1]{1,0,2:T(8,128)} %constant.163) | copy-start | bytes 772
  26.4 9.2 %collective-permute-start.3 = (f32[32,24]{0,1:T(8,128)S(1)}, f32[32,24]{0,1:T(8,128)S(1)}, u32[]{:S(2)}, u32[]{:S(2)}) collective-permute-start(f32[32,24]{0,1:T(8,128)S(1)} %get-tuple-element.107), channel_id=1, source_target_pairs={{1,0},{2,1},{3,2},{0,3},{5,4},{6,5},{7,6},{4,7},{9,8},{10,9},{11,1... | collective-permute-start | bytes 9224 | tf_op jit(solution)/shard_map/ppermute | solution.py:20
  30.2 3.9 %copy-start.16 = (f32[1,8,8,1280]{3,1,2,0:T(8,128)S(1)}, f32[1,8,8,1280]{3,1,2,0:T(8,128)}, u32[]{:S(2)}) copy-start(f32[1,8,8,1280]{3,1,2,0:T(8,128)} %get-tuple-element.106) | copy-start | bytes 983044
  30.2 3.9 %copy-start.17 = (f32[1,8,8,1280]{3,1,2,0:T(8,128)S(1)}, f32[1,8,8,1280]{3,1,2,0:T(8,128)}, u32[]{:S(2)}) copy-start(f32[1,8,8,1280]{3,1,2,0:T(8,128)} %get-tuple-element.122) | copy-start | bytes 983044
  30.4 3.6 %copy-start.12 = (f32[2,8,8,1280]{3,1,2,0:T(8,128)}, f32[2,8,8,1280]{3,1,2,0:T(8,128)S(1)}, u32[]{:S(2)}) copy-start(f32[2,8,8,1280]{3,1,2,0:T(8,128)S(1)} %copy.229) | copy-start | bytes 1966084
  34.1 1.5 %copy-start.5 = (f32[3,8,8,1280]{3,1,2,0:T(8,128)}, f32[3,8,8,1280]{3,1,2,0:T(8,128)S(1)}, u32[]{:S(2)}) copy-start(f32[3,8,8,1280]{3,1,2,0:T(8,128)S(1)} %maximum_multiply_fusion) | copy-start | bytes 2949124
  53.4 2.1 %copy-start.39 = (f32[8,8,1,1]{1,0,3,2:T(8,128)S(1)}, f32[8,8,1,1]{1,0,3,2:T(8,128)}, u32[]{:S(2)}) copy-start(f32[8,8,1,1]{1,0,3,2:T(8,128)} %constant.164) | copy-start | bytes 772
  53.4 2.8 %copy-start.26 = (pred[4,1280]{1,0:T(4,128)(4,1)S(1)}, pred[4,1280]{1,0:T(4,128)(4,1)}, u32[]{:S(2)}) copy-start(pred[4,1280]{1,0:T(4,128)(4,1)} %get-tuple-element.121) | copy-start | bytes 15364
  53.4 2.9 %copy-start.31 = (pred[4,1280]{1,0:T(4,128)(4,1)S(1)}, pred[4,1280]{1,0:T(4,128)(4,1)}, u32[]{:S(2)}) copy-start(pred[4,1280]{1,0:T(4,128)(4,1)} %get-tuple-element.120) | copy-start | bytes 15364
  53.4 2.9 %copy-start.38 = (f32[8,8,1,1]{1,0,3,2:T(8,128)S(1)}, f32[8,8,1,1]{1,0,3,2:T(8,128)}, u32[]{:S(2)}) copy-start(f32[8,8,1,1]{1,0,3,2:T(8,128)} %constant.165) | copy-start | bytes 772
  55.5 5.4 %copy-start.18 = (f32[1,1,8,1280]{3,2,1,0:T(8,128)S(1)}, f32[1,1,8,1280]{3,2,1,0:T(8,128)}, u32[]{:S(2)}) copy-start(f32[1,1,8,1280]{3,2,1,0:T(8,128)} %get-tuple-element.94) | copy-start | bytes 122884
  57.0 6.6 %copy-start.37 = (f32[8,8,1,1]{1,0,3,2:T(8,128)S(1)}, f32[8,8,1,1]{1,0,3,2:T(8,128)}, u32[]{:S(2)}) copy-start(f32[8,8,1,1]{1,0,3,2:T(8,128)} %constant.166) | copy-start | bytes 772
  58.0 6.2 %copy-start.36 = (f32[8,8,1,1]{1,0,3,2:T(8,128)S(1)}, f32[8,8,1,1]{1,0,3,2:T(8,128)}, u32[]{:S(2)}) copy-start(f32[8,8,1,1]{1,0,3,2:T(8,128)} %constant.167) | copy-start | bytes 772
  61.7 3.0 %copy-start.8 = (f32[3,8,1,1280]{3,1,0,2:T(8,128)}, f32[3,8,1,1280]{3,1,0,2:T(8,128)S(1)}, u32[]{:S(2)}) copy-start(f32[3,8,1,1280]{3,1,0,2:T(8,128)S(1)} %copy.233) | copy-start | bytes 368644
  63.5 1.2 copy-start.9
  63.5 1.2 copy-start.10
  63.6 1.2 copy-start.11
  67.0 5.8 %copy-start.19 = (f32[1,8,1280]{2,1,0:T(8,128)S(1)}, f32[1,8,1280]{2,1,0:T(8,128)}, u32[]{:S(2)}) copy-start(f32[1,8,1280]{2,1,0:T(8,128)} %slice_bitcast_fusion.5) | copy-start | bytes 122884
  67.0 5.8 %copy-start.23 = (f32[1,8,1280]{2,1,0:T(8,128)S(1)}, f32[1,8,1280]{2,1,0:T(8,128)}, u32[]{:S(2)}) copy-start(f32[1,8,1280]{2,1,0:T(8,128)} %get-tuple-element.85) | copy-start | bytes 122884
  67.0 6.5 %copy-start.21 = (f32[1,8,1280]{2,1,0:T(8,128)S(1)}, f32[1,8,1280]{2,1,0:T(8,128)}, u32[]{:S(2)}) copy-start(f32[1,8,1280]{2,1,0:T(8,128)} %get-tuple-element.84) | copy-start | bytes 122884
  67.0 6.5 %copy-start.22 = (f32[1,8,1280]{2,1,0:T(8,128)S(1)}, f32[1,8,1280]{2,1,0:T(8,128)}, u32[]{:S(2)}) copy-start(f32[1,8,1280]{2,1,0:T(8,128)} %get-tuple-element.92) | copy-start | bytes 122884
  67.0 7.1 %copy-start.20 = (f32[1,8,1280]{2,1,0:T(8,128)S(1)}, f32[1,8,1280]{2,1,0:T(8,128)}, u32[]{:S(2)}) copy-start(f32[1,8,1280]{2,1,0:T(8,128)} %get-tuple-element.95) | copy-start | bytes 122884
  67.0 19.2 %copy-start.25 = (s32[5120]{0:T(1024)S(1)}, s32[5120]{0:T(1024)}, u32[]{:S(2)}) copy-start(s32[5120]{0:T(1024)} %get-tuple-element.124) | copy-start | bytes 61444
  72.8 11.8 %collective-permute-start.4 = (f32[24,32]{0,1:T(8,128)S(1)}, f32[24,32]{0,1:T(8,128)S(1)}, u32[]{:S(2)}, u32[]{:S(2)}) collective-permute-start(f32[24,32]{0,1:T(8,128)S(1)} %get-tuple-element.114), channel_id=1, source_target_pairs={{124,0},{0,4},{4,8},{8,12},{12,16},{16,20},{20,24},{24,28},{28,32}... | collective-permute-start | bytes 9224 | tf_op jit(solution)/shard_map/ppermute | solution.py:20
  74.8 29.2 %copy-start.24 = (s32[5120]{0:T(1024)S(1)}, s32[5120]{0:T(1024)}, u32[]{:S(2)}) copy-start(s32[5120]{0:T(1024)} %get-tuple-element.123) | copy-start | bytes 61444
  76.3 8.3 %collective-permute-start.5 = (f32[24,32]{0,1:T(8,128)S(1)}, f32[24,32]{0,1:T(8,128)S(1)}, u32[]{:S(2)}, u32[]{:S(2)}) collective-permute-start(f32[24,32]{0,1:T(8,128)S(1)} %get-tuple-element.113), channel_id=1, source_target_pairs={{4,0},{8,4},{12,8},{16,12},{20,16},{24,20},{28,24},{32,28},{36,32}... | collective-permute-start | bytes 9224 | tf_op jit(solution)/shard_map/ppermute | solution.py:20
  81.3 4.9 %collective-permute-start.6 = (f32[24,16]{0,1:T(8,128)S(1)}, f32[24,16]{0,1:T(8,128)S(1)}, u32[]{:S(2)}, u32[]{:S(2)}) collective-permute-start(f32[24,16]{0,1:T(8,128)S(1)} %get-tuple-element.112), channel_id=1, source_target_pairs={{3,0},{0,1},{1,2},{2,3},{7,4},{4,5},{5,6},{6,7},{11,8},{8,9},{9,10... | collective-permute-start | bytes 4616 | tf_op jit(solution)/shard_map/ppermute | solution.py:20
  81.7 4.5 %collective-permute-start.7 = (f32[24,16]{0,1:T(8,128)S(1)}, f32[24,16]{0,1:T(8,128)S(1)}, u32[]{:S(2)}, u32[]{:S(2)}) collective-permute-start(f32[24,16]{0,1:T(8,128)S(1)} %get-tuple-element.111), channel_id=1, source_target_pairs={{1,0},{2,1},{3,2},{0,3},{5,4},{6,5},{7,6},{4,7},{9,8},{10,9},{11,1... | collective-permute-start | bytes 4616 | tf_op jit(solution)/shard_map/ppermute | solution.py:20
  125.3 2.8 %copy-start.6 = (f32[3,8,8,1280]{3,1,2,0:T(8,128)S(1)}, f32[3,8,8,1280]{3,1,2,0:T(8,128)}, u32[]{:S(2)}) copy-start(f32[3,8,8,1280]{3,1,2,0:T(8,128)} %copy-done.5) | copy-start | bytes 2949124
  125.5 12.3 %copy-start.3 = (f32[2,8,8,1280]{3,2,1,0:T(8,128)S(1)}, f32[2,8,8,1280]{3,2,1,0:T(8,128)}, u32[]{:S(2)}) copy-start(f32[2,8,8,1280]{3,2,1,0:T(8,128)} %param.23) | copy-start | bytes 1966084
  (2 other events, 2.0 us)
where the time goes:
time: 141 us; the launch traced here: 140 us
  local copies, waits for them, and re-layouts  87.9 us (62%)
  other arithmetic  26.5 us (19%)
  starting transfers between devices  17.7 us (13%)
  matrix products  4.67 us (3%)
  waiting for transfers between devices  1.62 us (1%)
  between operations  1.57 us (1%)
    gather x2, local copies, waits for them, and re-layouts, surface_fluxes(): trace_pool[:, trace_index.reshape(-1)].reshape(4, 8, 4, element_count)  19.9 us
    gather x1, local copies, waits for them, and re-layouts, mortar_from_pool(): pool_two[:, mortar_index[0].reshape(-1)]  17.8 us
    gather x1, local copies, waits for them, and re-layouts, mortar_from_pool(): pool_two[:, mortar_index[1].reshape(-1)]  17.7 us
    ppermute x8, starting transfers between devices, from_behind(): return lax.ppermute(block, axis, route)  17.7 us
    unnamed x105, local copies, waits for them, and re-layouts  8.79 us
    reduce_sum x1, other arithmetic, volume_rates(): rate_x = rate_x - jnp.sum(factor_y * pair_y[2], axis=2)  6.35 us
    scatter-add x1, local copies, waits for them, and re-layouts, finish_section(): rate_all = rate_all.at[:, 0].add(-lifted[:, :, 0])  4.61 us
    scatter-add x1, local copies, waits for them, and re-layouts, finish_section(): rate_all = rate_all.at[:, -1].add(-lifted[:, :, 1])  4.61 us
  transfers between devices with their start and end apart: 8, of which 1 were waited for; matrix products, arithmetic and copies ran while one was open for 8% of the time, Pallas kernels for 0%

commit v1 on v0

v1 whole, which is shorter than its diff:
```python
import jax
import jax.numpy as jnp
import numpy as np
from jax import lax
from jax.experimental import pallas as pl
from jax.experimental.pallas import tpu as pltpu
from jax.sharding import PartitionSpec as P

NODES = 8
ELEMS = 1280
LANES = 128
BLOCKS = ELEMS // LANES
TREE_BLOCKS = BLOCKS // 2
FACES = 4
STATE, TRACE, MOVED = 256, 128, 192
LOCAL = FACES * ELEMS
STEP = 0.005
F32 = jnp.float32
I32 = jnp.int32

SEND_AT = (0, 48, 96, 120)
SEND_CAP = (48, 48, 24, 24)
BACK_AT = (48, 96, 64, 80)
BACK_CAP = (32, 32, 16, 16)
RECV_OFF = (0, 48, 96, 120)
RECV_LANE = (48, 0, 120, 96)
RETN_OFF = (0, 32, 64, 80)
RETN_LANE = (96, 48, 80, 64)


def tables():
    degree = NODES - 1

    def legendre(points):
        before, current = np.ones(points.shape), points * 1.0
        for order in range(2, degree + 1):
            before, current = (
                current,
                ((2.0 * order - 1.0) * points * current - (order - 1.0) * before) / order,
            )
        return current, before

    points = -np.cos(np.pi * np.arange(NODES) / degree)
    for _ in range(100):
        top, below = legendre(points)
        points = points - (points * top - below) / (NODES * top)
    points[0], points[-1] = -1.0, 1.0
    values = legendre(points)[0]
    weights = 2.0 / (degree * NODES * values * values)
    deriv = np.zeros((NODES, NODES))
    for i in range(NODES):
        for k in range(NODES):
            if i != k:
                deriv[i, k] = values[i] / (values[k] * (points[i] - points[k]))

    def lagrange(targets):
        table = np.ones((NODES, NODES))
        for k in range(NODES):
            for o in range(NODES):
                if o != k:
                    table[:, k] = table[:, k] * (targets - points[o]) / (points[k] - points[o])
        return table

    low, high = lagrange((points - 1.0) / 2.0), lagrange((points + 1.0) / 2.0)
    proj_low = 0.5 * low.T * weights[None, :] / weights[:, None]
    proj_high = 0.5 * high.T * weights[None, :] / weights[:, None]
    return weights, deriv, low, high, proj_low, proj_high


WEIGHTS, DERIV, INTERP_LOW, INTERP_HIGH, PROJ_LOW, PROJ_HIGH = tables()
SKEW = WEIGHTS[:, None] * DERIV
LIFT = 1.0 / WEIGHTS[0]


def column_tables():
    stack = np.stack([INTERP_LOW, INTERP_HIGH, PROJ_LOW, PROJ_HIGH]).transpose(0, 2, 1)
    return np.broadcast_to(stack.reshape(4 * NODES * NODES, 1), (4 * NODES * NODES, LANES)).astype(
        np.float32
    )


def face_rows(base, face):
    if face == 0:
        return pl.ds(base, 8)
    if face == 1:
        return pl.ds(base + 56, 8)
    if face == 2:
        return pl.ds(base, 8, stride=8)
    return pl.ds(base + 7, 8, stride=8)


def lanes_of(block):
    return pl.ds(pl.multiple_of(block * LANES, LANES), LANES)


def spread(row):
    return jnp.broadcast_to(row, (8, LANES))


def pick(source, lane):
    return jnp.take_along_axis(source, lane, axis=1, mode="promise_in_bounds")


def pack_kernel(depth, moment, bed, send, back, state, traces, wide_a, wide_b, narrow_a, narrow_b, sems):
    copies = []
    for block in range(BLOCKS):
        lanes = pl.ds(block * LANES, LANES)
        base = block * STATE
        for slot, (source, row, count) in enumerate(
            ((depth, 0, 64), (moment, 64, 128), (bed, 192, 64))
        ):
            copies.append(
                pltpu.make_async_copy(
                    source.at[:, lanes], state.at[pl.ds(base + row, count)], sems.at[slot, block]
                )
            )
    for copy in copies:
        copy.start()
    lane_id = lax.broadcasted_iota(I32, (8, LANES), 1)
    send_first = spread(send[:, 0:LANES])
    send_last = spread(send[:, LANES : 2 * LANES])
    back_row = spread(back[:, 0:LANES])
    backs = (
        pltpu.roll(back_row, 48, 1),
        pltpu.roll(back_row, 64, 1),
        back_row,
        back_row,
    )
    index = []
    for way in range(4):
        row = send_first
        if way == 3:
            row = jnp.where(lane_id < 64, send_last, send_first)
        inside = (lane_id >= BACK_AT[way]) & (lane_id < BACK_AT[way] + BACK_CAP[way])
        row = jnp.where(inside, backs[way], row)
        index.append(row - way * ELEMS)
    for copy in copies:
        copy.wait()
    for block in range(BLOCKS):
        for face in range(FACES):
            for comp in range(4):
                traces[pl.ds(block * TRACE + (face * 4 + comp) * 8, 8), :] = state[
                    face_rows(block * STATE + comp * 64, face), :
                ]
    out = []
    for way in range(4):
        lane = index[way] & (LANES - 1)
        place = index[way] >> 7
        found = []
        for comp in range(4):
            base = (way * 4 + comp) * 8
            total = jnp.zeros((8, LANES), F32)
            for block in range(BLOCKS):
                got = pick(traces[pl.ds(block * TRACE + base, 8), :], lane)
                total = jnp.where(place == block, got, total)
            found.append(total)
        out.append(found)
    wide_even = (lax.axis_index("wide") & 1) == 0
    narrow_even = (lax.axis_index("narrow") & 1) == 0
    for comp in range(4):
        rows = pl.ds(comp * 8, 8)
        wide_a[rows, :] = jnp.where(wide_even, out[1][comp], out[0][comp])
        wide_b[rows, :] = jnp.where(wide_even, out[0][comp], out[1][comp])
        narrow_a[rows, :] = jnp.where(narrow_even, out[3][comp], out[2][comp])
        narrow_b[rows, :] = jnp.where(narrow_even, out[2][comp], out[3][comp])


def line_terms(height, normal, tangent, bed):
    square = [2.0 * h * h for h in height]
    mass = [None] * 8
    along = [None] * 8
    cross = [None] * 8
    slope = [None] * 8

    def add(slot, i, value):
        slot[i] = value if slot[i] is None else slot[i] + value

    def sub(slot, i, value):
        slot[i] = -value if slot[i] is None else slot[i] - value

    for i in range(8):
        for k in range(i + 1, 8):
            q = float(SKEW[i, k])
            un = normal[i] + normal[k]
            ut = tangent[i] + tangent[k]
            first = (q * (height[i] + height[k])) * un
            second = first * un + q * (square[i] + square[k])
            third = first * ut
            bump = q * (bed[k] - bed[i])
            add(mass, i, first)
            sub(mass, k, first)
            add(along, i, second)
            sub(along, k, second)
            add(cross, i, third)
            sub(cross, k, third)
            add(slope, i, bump)
            add(slope, k, bump)
    out = []
    for i in range(8):
        scale = STEP / WEIGHTS[i]
        out.append(
            (
                float(0.5 * scale) * mass[i],
                float(0.25 * scale) * (along[i] + (4.0 * height[i]) * slope[i]),
                float(0.25 * scale) * cross[i],
            )
        )
    return out


def volume_kernel(state, levels, moved, scratch):
    def body(block, carry):
        lanes = lanes_of(block)
        metric = spread((levels[:, lanes] + 1).astype(F32))
        base = pl.multiple_of(block * STATE, STATE)
        into = pl.multiple_of(block * MOVED, MOVED)

        def load(comp, j, across):
            if across:
                return state[pl.ds(base + comp * 64 + j, 8, stride=8), :]
            return state[pl.ds(base + comp * 64 + j * 8, 8), :]

        for across in (True, False):
            height = [load(0, j, across) for j in range(8)]
            inverse = [1.0 / h for h in height]
            vel_x = [load(1, j, across) * inverse[j] for j in range(8)]
            vel_y = [load(2, j, across) * inverse[j] for j in range(8)]
            bed = [load(3, j, across) for j in range(8)]
            if across:
                terms = line_terms(height, vel_y, vel_x, bed)
                for j in range(8):
                    mass, along, cross = terms[j]
                    scratch[pl.ds(j, 8, stride=8), :] = mass
                    scratch[pl.ds(64 + j, 8, stride=8), :] = cross
                    scratch[pl.ds(128 + j, 8, stride=8), :] = along
            else:
                terms = line_terms(height, vel_x, vel_y, bed)
                for i in range(8):
                    mass, along, cross = terms[i]
                    for comp, value in enumerate((mass, along, cross)):
                        row = comp * 64 + i * 8
                        moved[pl.ds(into + row, 8), :] = state[pl.ds(base + row, 8), :] - metric * (
                            value + scratch[pl.ds(row, 8), :]
                        )
        return carry

    lax.fori_loop(0, BLOCKS, body, 0)


def apply(table, pieces):
    total = None
    for node in range(8):
        term = table[node] * spread(pieces[node : node + 1, :])
        total = term if total is None else total + term
    return total


def numeric_flux(left, right, sign):
    inv_l, inv_r = 1.0 / left[0], 1.0 / right[0]
    un_l, un_r = left[1] * inv_l, right[1] * inv_r
    ut_l, ut_r = left[2] * inv_l, right[2] * inv_r
    un = un_l + un_r
    ut = ut_l + ut_r
    speed = jnp.maximum(
        jnp.abs(un_l) + jnp.sqrt(left[0]), jnp.abs(un_r) + jnp.sqrt(right[0])
    )
    half = 0.5 * speed
    first = (0.25 * sign) * (left[0] + right[0]) * un
    second = 0.5 * (first * un) + (0.25 * sign) * (left[0] * left[0] + right[0] * right[0])
    third = 0.5 * (first * ut)
    return (
        first - half * ((right[0] + right[3]) - (left[0] + left[3])),
        second - half * (right[1] - left[1]),
        third - half * (right[2] - left[2]),
    )


def surface_kernel(
    moved, traces, got_wa, got_wb, got_na, got_nb, kinds, trace_src, mortar_src, levels, table_ref,
    new_depth, new_moment, result, sems
):
    wide_even = (lax.axis_index("wide") & 1) == 0
    narrow_even = (lax.axis_index("narrow") & 1) == 0

    def came(face, comp):
        rows = pl.ds(comp * 8, 8)
        if face == 0:
            return jnp.where(wide_even, got_wb[rows, :], got_wa[rows, :])
        if face == 1:
            return jnp.where(wide_even, got_wa[rows, :], got_wb[rows, :])
        if face == 2:
            return jnp.where(narrow_even, got_nb[rows, :], got_na[rows, :])
        return jnp.where(narrow_even, got_na[rows, :], got_nb[rows, :])

    def table(which, node):
        return table_ref[pl.ds((which * 8 + node) * 8, 8), :]

    def copies(block):
        lanes = lanes_of(block)
        row = pl.multiple_of(block * MOVED, MOVED)
        return (
            pltpu.make_async_copy(
                result.at[pl.ds(row, 64)], new_depth.at[:, lanes], sems.at[0, block]
            ),
            pltpu.make_async_copy(
                result.at[pl.ds(row + 64, 128)], new_moment.at[:, lanes], sems.at[1, block]
            ),
        )

    def body(block, carry):
        lanes = lanes_of(block)
        into = pl.multiple_of(block * MOVED, MOVED)
        held = pl.multiple_of(block * TRACE, TRACE)
        for row in range(24):
            rows = pl.ds(into + row * 8, 8)
            result[rows, :] = moved[rows, :]
        factor = spread((levels[:, lanes] + 1).astype(F32)) * float(LIFT * STEP)
        for face in range(FACES):
            opposite = face ^ 1
            kind = spread(kinds[face : face + 1, lanes])
            fine_low = spread(mortar_src[face : face + 1, lanes])
            fine_high = spread(mortar_src[4 + face : 5 + face, lanes])
            source = spread(trace_src[face : face + 1, lanes])
            coarse = kind == 3
            first = jnp.where(coarse, fine_low, source)
            back_shift = RETN_LANE[face] - RETN_OFF[face] - LOCAL
            shift = jnp.where(coarse, back_shift, RECV_LANE[face] - RECV_OFF[face] - LOCAL)
            first_far = first >= LOCAL
            high_far = fine_high >= LOCAL
            first = first + jnp.where(first_far, shift, -opposite * ELEMS)
            high = fine_high + jnp.where(high_far, back_shift, -opposite * ELEMS)
            first_place = jnp.where(first_far, BLOCKS, first >> 7)
            high_place = jnp.where(high_far, BLOCKS, high >> 7)
            first_lane = first & (LANES - 1)
            high_lane = high & (LANES - 1)
            near = []
            above = []
            for comp in range(4):
                base = (opposite * 4 + comp) * 8
                arrived = came(face, comp)
                one = pick(arrived, first_lane)
                two = pick(arrived, high_lane)
                for other in range(BLOCKS):
                    piece = traces[pl.ds(other * TRACE + base, 8), :]
                    one = jnp.where(first_place == other, pick(piece, first_lane), one)
                    two = jnp.where(high_place == other, pick(piece, high_lane), two)
                near.append(one)
                above.append(two)
            own = [traces[pl.ds(held + (face * 4 + comp) * 8, 8), :] for comp in range(4)]
            blend = [jnp.where(coarse, own[c], near[c]) for c in range(4)]
            low = [apply([table(0, n) for n in range(8)], b) for b in blend]
            high_of = [apply([table(1, n) for n in range(8)], b) for b in blend]
            left = [jnp.where(coarse, low[c], own[c]) for c in range(4)]
            right = [
                jnp.where(kind == 1, low[c], jnp.where(kind == 2, high_of[c], near[c]))
                for c in range(4)
            ]
            order = (0, 1, 2, 3) if face < 2 else (0, 2, 1, 3)
            sign = -1.0 if face % 2 == 0 else 1.0
            flux = numeric_flux([left[c] for c in order], [right[c] for c in order], sign)
            extra = numeric_flux([high_of[c] for c in order], [above[c] for c in order], sign)
            order = order[:3]
            for comp in range(3):
                one, two = flux[order[comp]], extra[order[comp]]
                joined = apply([table(2, n) for n in range(8)], one) + apply(
                    [table(3, n) for n in range(8)], two
                )
                change = factor * jnp.where(coarse, joined, one)
                rows = face_rows(into + comp * 64, face)
                result[rows, :] = result[rows, :] - change
        for copy in copies(block):
            copy.start()
        return carry

    lax.fori_loop(0, BLOCKS, body, 0)

    def finish(block, carry):
        for copy in copies(block):
            copy.wait()
        return carry

    lax.fori_loop(0, BLOCKS, finish, 0)


VM = pl.BlockSpec(memory_space=pltpu.VMEM)
ANY = pl.BlockSpec(memory_space=pl.ANY)


def swap(block, axis, phase):
    size = lax.axis_size(axis)
    route = [(i, (((i + phase) ^ 1) - phase) % size) for i in range(size)]
    return lax.ppermute(block, axis, route)


def on_device(depth, momentum, bed, levels, kinds, send, trace_src, back, mortar_src):
    depth = depth.reshape(64, ELEMS)
    momentum = momentum.reshape(128, ELEMS)
    bed = bed.reshape(64, ELEMS)
    levels = levels.reshape(1, ELEMS)
    mortar_src = mortar_src.reshape(8, ELEMS)
    send = jnp.pad(send, (0, 112)).reshape(1, 256)
    back = jnp.pad(back, (0, 32)).reshape(1, 128)
    message = jax.ShapeDtypeStruct((32, LANES), F32)
    state, traces, wide_a, wide_b, narrow_a, narrow_b = pl.pallas_call(
        pack_kernel,
        out_shape=(
            jax.ShapeDtypeStruct((BLOCKS * STATE, LANES), F32),
            jax.ShapeDtypeStruct((BLOCKS * TRACE, LANES), F32),
            message,
            message,
            message,
            message,
        ),
        in_specs=[ANY, ANY, ANY, VM, VM],
        out_specs=[VM] * 6,
        scratch_shapes=[pltpu.SemaphoreType.DMA((3, BLOCKS))],
        name="pack",
    )(depth, momentum, bed, send, back)
    got_wb = swap(wide_b, "wide", 1)
    got_na = swap(narrow_a, "narrow", 0)
    got_nb = swap(narrow_b, "narrow", 1)
    got_wa = swap(wide_a, "wide", 0)
    moved = pl.pallas_call(
        volume_kernel,
        out_shape=jax.ShapeDtypeStruct((BLOCKS * MOVED, LANES), F32),
        in_specs=[VM, VM],
        out_specs=VM,
        scratch_shapes=[pltpu.VMEM((192, LANES), F32)],
        name="volume",
        cost_estimate=pl.CostEstimate(flops=20_000_000, bytes_accessed=2_000_000, transcendentals=0),
    )(state, levels)
    new_depth, new_moment = pl.pallas_call(
        surface_kernel,
        out_shape=(
            jax.ShapeDtypeStruct((64, ELEMS), F32),
            jax.ShapeDtypeStruct((128, ELEMS), F32),
        ),
        in_specs=[VM] * 11,
        out_specs=[ANY, ANY],
        scratch_shapes=[pltpu.VMEM((BLOCKS * MOVED, LANES), F32), pltpu.SemaphoreType.DMA((2, BLOCKS))],
        name="surface",
    )(
        moved, traces, got_wa, got_wb, got_na, got_nb, kinds, trace_src, mortar_src, levels,
        jnp.asarray(column_tables()),
    )
    return new_depth.reshape(8, 8, ELEMS), new_moment.reshape(2, 8, 8, ELEMS)


def solution(mesh):
    both = ("wide", "narrow")
    placed = (
        P(None, None, both),
        P(None, None, None, both),
        P(None, None, both),
        P(both),
        P(None, both),
        P(both),
        P(None, both),
        P(both),
        P(None, None, both),
    )
    return jax.shard_map(
        on_device,
        mesh=mesh,
        in_specs=placed,
        out_specs=(P(None, None, both), P(None, None, None, both)),
        check_vma=False,
    )
```

time: 141 us -> 33 us (0.23)
  local copies, waits for them, and re-layouts: 87.9 us -> 4.26 us
  other arithmetic: 26.5 us -> 0 us
  Pallas kernels: 0 us -> 17.4 us
  starting transfers between devices: 17.7 us -> 10.3 us
  matrix products: 4.67 us -> 0 us
  waiting for transfers between devices: 1.62 us -> 0.01 us
    gather x6 -> x0, local copies, waits for them, and re-layouts: 59.1 us -> none  [the longest x2 19.9 us: surface_fluxes(): trace_pool[:, trace_index.reshape(-1)].reshape(4, 8, 4, element_count)]
    pallas_call x0 -> x3, Pallas kernels: none -> 17.4 us  [the longest x1 9.54 us: on_device(): pl.pallas_call(surface_kernel, out_shape=(jax.ShapeDtypeStruct((64, ELEMS...]
    scatter-add x2 -> x0, local copies, waits for them, and re-layouts: 9.23 us -> none  [the longest x1 4.61 us: finish_section(): rate_all = rate_all.at[:, 0].add(-lifted[:, :, 0])]
    unnamed x105 -> x12, local copies, waits for them, and re-layouts: 8.79 us -> 0.6 us
    ppermute x8 -> x4, starting transfers between devices: 17.7 us -> 10.3 us  [swap(): return lax.ppermute(block, axis, route)]
    reduce_sum x1 -> x0, other arithmetic: 6.35 us -> none  [volume_rates(): rate_x = rate_x - jnp.sum(factor_y * pair_y[2], axis=2)]
    sub x6 -> x0, other arithmetic: 6.2 us -> none  [the longest x3 3.23 us: face_flux(): normal_sign * flux_mass]
    dot_general x6 -> x0, matrix products: 4.67 us -> none  [the longest x1 1.52 us: volume_rates(): slope_y = jnp.einsum('jk,ike->ije', derivative, bed, precision=highest)]
  transfers between devices with their start and end apart: 8 -> 4, of which waited for: 1 -> 0; matrix products, arithmetic and copies ran while one was open for 8% -> 4% of each run, Pallas kernels for 0% -> 13%
where the time goes in v1:
time: 33 us; the launch traced here: 32.7 us
  Pallas kernels  17.4 us (53%)
  starting transfers between devices  10.3 us (31%)
  local copies, waits for them, and re-layouts  4.26 us (13%)
  between operations  0.71 us (2%)
    ppermute x4, starting transfers between devices, swap(): return lax.ppermute(block, axis, route)  10.3 us
    pallas_call x1, Pallas kernels, on_device(): pl.pallas_call(surface_kernel, out_shape=(jax.ShapeDtypeStruct((64, ELEMS...  9.54 us
    pallas_call x1, Pallas kernels, on_device(): pl.pallas_call(volume_kernel, out_shape=jax.ShapeDtypeStruct((BLOCKS * MO...  4.31 us
    pallas_call x1, Pallas kernels, on_device(): pl.pallas_call(pack_kernel, out_shape=(jax.ShapeDtypeStruct((BLOCKS * STA...  3.56 us
    pad x1, local copies, waits for them, and re-layouts, on_device(): send = jnp.pad(send, (0, 112)).reshape(1, 256)  1.26 us
    reshape x1, local copies, waits for them, and re-layouts, on_device(): back = jnp.pad(back, (0, 32)).reshape(1, 128)  1.19 us
  transfers between devices with their start and end apart: 4, of which 0 were waited for; matrix products, arithmetic and copies ran while one was open for 4% of the time, Pallas kernels for 13%

profile of v1, /device:TPU:0, one launch (start us, length us, event | category | flops | bytes accessed | tf_op | source)
XLA Modules:
  0.0 32.7 jit_solution(274147849272764647)
XLA Ops:
  0.6 0.0 copy-start.5
  0.6 0.0 copy-start
  0.7 1.2 %pad_bitcast_fusion.back = s32[1,128]{1,0:T(1,128)} fusion(s32[96]{0:T(128)} %param.17), kind=kLoop, calls=%fused_computation | loop fusion | bytes 896 | tf_op jit(solution)/shard_map/reshape | solution.py:402
  1.8 1.3 %pad.8 = s32[256]{0:T(256)} pad(s32[144]{0:T(256)} %param.15, s32[]{:T(128)} %constant.1.clone.1), padding=0_112 | pad | bytes 1604 | tf_op jit(solution)/shard_map/jit(_pad)/pad | solution.py:401
  3.1 3.6 %pack.1 = (f32[2560,128]{1,0:T(8,128)}, f32[1280,128]{1,0:T(8,128)}, f32[32,128]{1,0:T(8,128)}, f32[32,128]{1,0:T(8,128)}, f32[32,128]{1,0:T(8,128)}, /*index=5*/f32[32,128]{1,0:T(8,128)}) custom-call(f32[64,1280]{1,0:T(8,128)} %bitcast.9, f32[128,1280]{1,0:T(8,128)} %bitcast.8, f32[64,1280]{1,0:T(8,128)} %bitcast.10, s32[1,256]{1,0:T(1,128)} %bitcast.11, ...), custom_call_target="tpu_custom_call" | custom-call | tf_op jit(solution)/shard_map/pack/pallas_call | solution.py:404
  6.7 0.1 collective-permute-start
  6.8 6.4 %collective-permute-start.1 = (f32[32,128]{1,0:T(8,128)}, f32[32,128]{1,0:T(8,128)S(1)}, u32[]{:S(2)}, u32[]{:S(2)}) collective-permute-start(f32[32,128]{1,0:T(8,128)} %get-tuple-element.13), channel_id=1, source_target_pairs={{0,124},{4,8},{8,4},{12,16},{16,12},{20,24},{24,20},{28,32},{32,28... | collective-permute-start | bytes 49160 | tf_op jit(solution)/shard_map/ppermute | solution.py:392
  13.2 1.6 %collective-permute-start.2 = (f32[32,128]{1,0:T(8,128)}, f32[32,128]{1,0:T(8,128)S(1)}, u32[]{:S(2)}, u32[]{:S(2)}) collective-permute-start(f32[32,128]{1,0:T(8,128)} %get-tuple-element.14), channel_id=1, source_target_pairs={{0,1},{1,0},{2,3},{3,2},{4,5},{5,4},{6,7},{7,6},{8,9},{9,8},{10,11... | collective-permute-start | bytes 49160 | tf_op jit(solution)/shard_map/ppermute | solution.py:392
  14.8 2.2 %collective-permute-start.3 = (f32[32,128]{1,0:T(8,128)}, f32[32,128]{1,0:T(8,128)S(1)}, u32[]{:S(2)}, u32[]{:S(2)}) collective-permute-start(f32[32,128]{1,0:T(8,128)} %get-tuple-element.15), channel_id=1, source_target_pairs={{0,3},{1,2},{2,1},{3,0},{4,7},{5,6},{6,5},{7,4},{8,11},{9,10},{10,... | collective-permute-start | bytes 49160 | tf_op jit(solution)/shard_map/ppermute | solution.py:392
  16.9 0.0 copy-done.5
  16.9 0.6 %reshape.36.levels = s32[1,1280]{1,0:T(1,128)} reshape(s32[1280]{0:T(1024)S(1)} %copy-done.5) | data formatting | bytes 10240 | tf_op jit(solution)/shard_map/reshape | solution.py:399
  17.5 0.0 copy-done
  17.5 0.6 %reshape.37.mortar_src = s32[8,1280]{1,0:T(8,128)} reshape(s32[2,4,1280]{2,1,0:T(4,128)S(1)} %copy-done) | data formatting | bytes 81920 | tf_op jit(solution)/shard_map/reshape | solution.py:400
  18.1 4.3 %volume.1.moved = f32[1920,128]{1,0:T(8,128)} custom-call(f32[2560,128]{1,0:T(8,128)} %get-tuple-element.10.state, s32[1,1280]{1,0:T(1,128)} %reshape.36.levels), custom_call_target="tpu_custom_call" | custom-call | flops 20000000 | bytes 2000000 | tf_op jit(solution)/shard_map/volume/pallas_call | solution.py:423
  22.5 0.0 collective-permute-done.got_wa
  22.5 0.0 copy-start.1
  22.5 0.0 collective-permute-done.1.got_wb
  22.5 0.0 copy-start.2
  22.5 0.0 collective-permute-done.2.got_na
  22.5 0.0 copy-start.3
  22.5 0.0 collective-permute-done.3.got_nb
  22.5 0.0 copy-start.4
  22.5 0.5 %copy-done.1 = f32[32,128]{1,0:T(8,128)} copy-done((f32[32,128]{1,0:T(8,128)}, f32[32,128]{1,0:T(8,128)S(1)}, u32[]{:S(2)}) %copy-start.1) | copy-done | bytes 16408
  23.1 0.0 copy-done.2
  23.1 0.0 copy-done.3
  23.1 0.0 copy-done.4
  23.1 9.5 %surface.1 = (f32[64,1280]{1,0:T(8,128)}, f32[128,1280]{1,0:T(8,128)}) custom-call(f32[1920,128]{1,0:T(8,128)} %volume.1.moved, f32[1280,128]{1,0:T(8,128)} %get-tuple-element.11.traces, f32[32,128]{1,0:T(8,128)} %copy-done.1, f32[32,128]{1,0:T(8,128)} %copy-done.2, f32[32,128]{1,0:T(8,128)} %copy-done.3, f32[32,128]{1,0:T(8,128)} %copy-done.4, ...), custom_call_target="tpu_custom_call" | custom-call | tf_op jit(solution)/shard_map/surface/pallas_call | solution.py:432
Async XLA Ops:
  0.6 16.3 %copy-start.5 = (s32[1280]{0:T(1024)S(1)}, s32[1280]{0:T(1024)}, u32[]{:S(2)}) copy-start(s32[1280]{0:T(1024)} %param.13) | copy-start | bytes 15364
  0.6 16.9 %copy-start = (s32[2,4,1280]{2,1,0:T(4,128)S(1)}, s32[2,4,1280]{2,1,0:T(4,128)}, u32[]{:S(2)}) copy-start(s32[2,4,1280]{2,1,0:T(4,128)} %param.18) | copy-start | bytes 122884
  6.7 15.8 %collective-permute-start = (f32[32,128]{1,0:T(8,128)}, f32[32,128]{1,0:T(8,128)S(1)}, u32[]{:S(2)}, u32[]{:S(2)}) collective-permute-start(f32[32,128]{1,0:T(8,128)} %get-tuple-element.12), channel_id=1, source_target_pairs={{0,4},{4,0},{8,12},{12,8},{16,20},{20,16},{24,28},{28,24},{32,36},... | collective-permute-start | bytes 49160 | tf_op jit(solution)/shard_map/ppermute | solution.py:392
  6.8 15.7 %collective-permute-start.1 = (f32[32,128]{1,0:T(8,128)}, f32[32,128]{1,0:T(8,128)S(1)}, u32[]{:S(2)}, u32[]{:S(2)}) collective-permute-start(f32[32,128]{1,0:T(8,128)} %get-tuple-element.13), channel_id=1, source_target_pairs={{0,124},{4,8},{8,4},{12,16},{16,12},{20,24},{24,20},{28,32},{32,28... | collective-permute-start | bytes 49160 | tf_op jit(solution)/shard_map/ppermute | solution.py:392
  13.2 9.3 %collective-permute-start.2 = (f32[32,128]{1,0:T(8,128)}, f32[32,128]{1,0:T(8,128)S(1)}, u32[]{:S(2)}, u32[]{:S(2)}) collective-permute-start(f32[32,128]{1,0:T(8,128)} %get-tuple-element.14), channel_id=1, source_target_pairs={{0,1},{1,0},{2,3},{3,2},{4,5},{5,4},{6,7},{7,6},{8,9},{9,8},{10,11... | collective-permute-start | bytes 49160 | tf_op jit(solution)/shard_map/ppermute | solution.py:392
  14.8 7.8 %collective-permute-start.3 = (f32[32,128]{1,0:T(8,128)}, f32[32,128]{1,0:T(8,128)S(1)}, u32[]{:S(2)}, u32[]{:S(2)}) collective-permute-start(f32[32,128]{1,0:T(8,128)} %get-tuple-element.15), channel_id=1, source_target_pairs={{0,3},{1,2},{2,1},{3,0},{4,7},{5,6},{6,5},{7,4},{8,11},{9,10},{10,... | collective-permute-start | bytes 49160 | tf_op jit(solution)/shard_map/ppermute | solution.py:392
  22.5 0.6 %copy-start.1 = (f32[32,128]{1,0:T(8,128)}, f32[32,128]{1,0:T(8,128)S(1)}, u32[]{:S(2)}) copy-start(f32[32,128]{1,0:T(8,128)S(1)} %collective-permute-done.got_wa) | copy-start | bytes 49156
  22.5 0.6 %copy-start.2 = (f32[32,128]{1,0:T(8,128)}, f32[32,128]{1,0:T(8,128)S(1)}, u32[]{:S(2)}) copy-start(f32[32,128]{1,0:T(8,128)S(1)} %collective-permute-done.1.got_wb) | copy-start | bytes 49156
  22.5 0.6 %copy-start.3 = (f32[32,128]{1,0:T(8,128)}, f32[32,128]{1,0:T(8,128)S(1)}, u32[]{:S(2)}) copy-start(f32[32,128]{1,0:T(8,128)S(1)} %collective-permute-done.2.got_na) | copy-start | bytes 49156
  22.5 0.6 %copy-start.4 = (f32[32,128]{1,0:T(8,128)}, f32[32,128]{1,0:T(8,128)S(1)}, u32[]{:S(2)}) copy-start(f32[32,128]{1,0:T(8,128)S(1)} %collective-permute-done.3.got_nb) | copy-start | bytes 49156

commit v2 on v1

v2 whole, which is shorter than its diff:
```python
import jax
import jax.numpy as jnp
import numpy as np
from jax import lax
from jax.experimental import pallas as pl
from jax.experimental.pallas import tpu as pltpu
from jax.sharding import PartitionSpec as P

NODES = 8
ELEMS = 1280
LANES = 128
BLOCKS = ELEMS // LANES
TREE_BLOCKS = BLOCKS // 2
GROUPS = BLOCKS // 2
FACES = 4
STATE, TRACE, MOVED = 256, 128, 192
LOCAL = FACES * ELEMS
STEP = 0.005
F32 = jnp.float32
I32 = jnp.int32

SEND_AT = (0, 48, 96, 120)
SEND_CAP = (48, 48, 24, 24)
BACK_AT = (48, 96, 64, 80)
BACK_CAP = (32, 32, 16, 16)
RECV_OFF = (0, 48, 96, 120)
RECV_LANE = (48, 0, 120, 96)
RETN_OFF = (0, 32, 64, 80)
RETN_LANE = (96, 48, 80, 64)


def tables():
    degree = NODES - 1

    def legendre(points):
        before, current = np.ones(points.shape), points * 1.0
        for order in range(2, degree + 1):
            before, current = (
                current,
                ((2.0 * order - 1.0) * points * current - (order - 1.0) * before) / order,
            )
        return current, before

    points = -np.cos(np.pi * np.arange(NODES) / degree)
    for _ in range(100):
        top, below = legendre(points)
        points = points - (points * top - below) / (NODES * top)
    points[0], points[-1] = -1.0, 1.0
    values = legendre(points)[0]
    weights = 2.0 / (degree * NODES * values * values)
    deriv = np.zeros((NODES, NODES))
    for i in range(NODES):
        for k in range(NODES):
            if i != k:
                deriv[i, k] = values[i] / (values[k] * (points[i] - points[k]))

    def lagrange(targets):
        table = np.ones((NODES, NODES))
        for k in range(NODES):
            for o in range(NODES):
                if o != k:
                    table[:, k] = table[:, k] * (targets - points[o]) / (points[k] - points[o])
        return table

    low, high = lagrange((points - 1.0) / 2.0), lagrange((points + 1.0) / 2.0)
    proj_low = 0.5 * low.T * weights[None, :] / weights[:, None]
    proj_high = 0.5 * high.T * weights[None, :] / weights[:, None]
    return weights, deriv, low, high, proj_low, proj_high


WEIGHTS, DERIV, INTERP_LOW, INTERP_HIGH, PROJ_LOW, PROJ_HIGH = tables()
SKEW = WEIGHTS[:, None] * DERIV
LIFT = 1.0 / WEIGHTS[0]


FOLD_EVEN = 0.5 * (INTERP_LOW + INTERP_LOW[:, ::-1])[:, :4]
FOLD_ODD = 0.5 * (INTERP_LOW - INTERP_LOW[:, ::-1])[:, :4]
JOIN_SUM = 0.5 * (PROJ_LOW + PROJ_LOW[::-1])[:4]
JOIN_DIFF = 0.5 * (PROJ_LOW - PROJ_LOW[::-1])[:4]


def face_rows(base, face):
    if face == 0:
        return pl.ds(base, 8)
    if face == 1:
        return pl.ds(base + 56, 8)
    if face == 2:
        return pl.ds(base, 8, stride=8)
    return pl.ds(base + 7, 8, stride=8)


def component(face, place):
    return place if face < 2 or place in (0, 3) else 3 - place


def lanes_of(block):
    return pl.ds(pl.multiple_of(block * LANES, LANES), LANES)


def rows_of(base, count):
    return pl.ds(pl.multiple_of(base, 8), count)


def spread(row):
    return jnp.broadcast_to(row, (8, LANES))


def pick(source, lane):
    return jnp.take_along_axis(source, lane, axis=1, mode="promise_in_bounds")


def pack_kernel(
    depth, moment, bed, send, back, state, traces, wide_a, narrow_b, narrow_a, wide_b,
    send_list, back_list, sems, list_sems
):
    list_copies = [
        pltpu.make_async_copy(send, send_list, list_sems.at[0]),
        pltpu.make_async_copy(back, back_list, list_sems.at[1]),
    ]
    for copy in list_copies:
        copy.start()
    copies = []
    for block in range(BLOCKS):
        lanes = pl.ds(block * LANES, LANES)
        base = block * STATE
        for slot, (source, row, count) in enumerate(
            ((depth, 0, 64), (moment, 64, 128), (bed, 192, 64))
        ):
            copy = pltpu.make_async_copy(
                source.at[:, lanes], state.at[pl.ds(base + row, count)], sems.at[slot, block]
            )
            copy.start()
            copies.append(copy)
    for copy in list_copies:
        copy.wait()
    lane_id = lax.broadcasted_iota(I32, (8, LANES), 1)
    def full(row):
        row = row.reshape(1, row.shape[0])
        return spread(jnp.concatenate([row, jnp.zeros((1, LANES - row.shape[1]), I32)], axis=1))

    send_first = spread(send_list[pl.ds(0, LANES)].reshape(1, LANES))
    send_last = full(send_list[pl.ds(LANES, 16)])
    back_row = full(back_list[...])
    backs = (pltpu.roll(back_row, 48, 1), pltpu.roll(back_row, 64, 1), back_row, back_row)
    index = []
    for way in range(4):
        row = send_first
        if way == 3:
            row = jnp.where(lane_id < 64, send_last, send_first)
        inside = (lane_id >= BACK_AT[way]) & (lane_id < BACK_AT[way] + BACK_CAP[way])
        row = jnp.where(inside, backs[way], row)
        index.append(row - way * ELEMS)
    out = [[jnp.zeros((8, LANES), F32) for _ in range(4)] for _ in range(4)]
    lane = [row & (LANES - 1) for row in index]
    place = [row >> 7 for row in index]
    for block in range(BLOCKS):
        for copy in copies[3 * block : 3 * block + 3]:
            copy.wait()
        for way in range(4):
            here = place[way] == block
            for comp in range(4):
                piece = state[face_rows(block * STATE + component(way, comp) * 64, way), :]
                traces[pl.ds(block * TRACE + (way * 4 + comp) * 8, 8), :] = piece
                out[way][comp] = jnp.where(here, pick(piece, lane[way]), out[way][comp])
    wide_even = (lax.axis_index("wide") & 1) == 0
    narrow_even = (lax.axis_index("narrow") & 1) == 0
    for comp in range(4):
        rows = pl.ds(comp * 8, 8)
        wide_a[rows, :] = jnp.where(wide_even, out[1][comp], out[0][comp])
        wide_b[rows, :] = jnp.where(wide_even, out[0][comp], out[1][comp])
        narrow_a[rows, :] = jnp.where(narrow_even, out[3][comp], out[2][comp])
        narrow_b[rows, :] = jnp.where(narrow_even, out[2][comp], out[3][comp])


def line_terms(height, normal, tangent, bed):
    def accumulate(slot, i, value, minus=False):
        if slot[i] is None:
            slot[i] = -value if minus else value
        else:
            slot[i] = slot[i] - value if minus else slot[i] + value

    slope = [None] * 8
    for i in range(8):
        for k in range(i + 1, 8):
            bump = float(SKEW[i, k]) * (bed[k] - bed[i])
            accumulate(slope, i, bump)
            accumulate(slope, k, bump)
    square = [2.0 * (h * h) for h in height]
    mass = [None] * 8
    along = [(4.0 * height[i]) * slope[i] for i in range(8)]
    cross = [None] * 8
    for i in range(8):
        for k in range(i + 1, 8):
            q = float(SKEW[i, k])
            un = normal[i] + normal[k]
            first = (q * (height[i] + height[k])) * un
            second = first * un + q * (square[i] + square[k])
            third = first * (tangent[i] + tangent[k])
            for slot, value in ((mass, first), (along, second), (cross, third)):
                accumulate(slot, i, value)
                accumulate(slot, k, value, True)
    out = []
    for i in range(8):
        scale = STEP / WEIGHTS[i]
        out.append(
            (float(0.5 * scale) * mass[i], float(0.25 * scale) * along[i], float(0.25 * scale) * cross[i])
        )
    return out


def volume_of(state, moved, speeds, base, into, metric):
    def rows(comp, j, across):
        if across:
            return pl.ds(comp * 64 + j, 8, stride=8)
        return pl.ds(comp * 64 + j * 8, 8)

    def at(start, window):
        return pl.ds(start + window.start, window.size, window.stride)

    height = [state[at(base, rows(0, j, False)), :] for j in range(8)]
    bed = [state[at(base, rows(3, j, False)), :] for j in range(8)]
    vel_x, vel_y = [], []
    for j in range(8):
        inverse = 1.0 / height[j]
        vel_x.append(state[at(base, rows(1, j, False)), :] * inverse)
        vel_y.append(state[at(base, rows(2, j, False)), :] * inverse)
        speeds[rows(0, j, False), :] = vel_x[j]
        speeds[rows(1, j, False), :] = vel_y[j]
    terms = line_terms(height, vel_x, vel_y, bed)
    for i in range(8):
        for comp, value in enumerate(terms[i]):
            moved[at(into, rows(comp, i, False)), :] = (
                state[at(base, rows(comp, i, False)), :] - metric * value
            )
    height = [state[at(base, rows(0, j, True)), :] for j in range(8)]
    bed = [state[at(base, rows(3, j, True)), :] for j in range(8)]
    vel_x = [speeds[rows(0, j, True), :] for j in range(8)]
    vel_y = [speeds[rows(1, j, True), :] for j in range(8)]
    terms = line_terms(height, vel_y, vel_x, bed)
    for j in range(8):
        mass, along, cross = terms[j]
        for comp, value in enumerate((mass, cross, along)):
            window = at(into, rows(comp, j, True))
            moved[window, :] = moved[window, :] - metric * value


def interior_kernel(
    state, traces, kinds, trace_src, mortar_src, levels, moved, found, codes, rows_kind, rows_factor,
    speeds, picks
):
    face_id = lax.broadcasted_iota(I32, (4, LANES), 0)

    def by_face(values):
        total = jnp.full((4, LANES), values[3], I32)
        for face in range(3):
            total = jnp.where(face_id == face, values[face], total)
        return total

    home = by_face([-(face ^ 1) * ELEMS for face in range(FACES)])
    recv_shift = by_face([RECV_LANE[f] - RECV_OFF[f] - LOCAL for f in range(FACES)])
    retn_shift = by_face([RETN_LANE[f] - RETN_OFF[f] - LOCAL for f in range(FACES)])

    for tree in range(2):

        def body(step, carry, tree=tree):
            block = step + tree * TREE_BLOCKS
            lanes = lanes_of(block)
            base = pl.multiple_of(block * STATE, STATE)
            into = pl.multiple_of(block * MOVED, MOVED)
            level_row = (levels[lanes].reshape(1, LANES) + 1).astype(F32)
            kind = kinds[:, lanes]
            coarse = kind == 3
            first = jnp.where(coarse, mortar_src[0, :, lanes], trace_src[:, lanes])
            second = mortar_src[1, :, lanes]
            four = pl.ds(pl.multiple_of(block * 4, 4), 4)
            for turn, (index, shift) in enumerate(
                ((first, jnp.where(coarse, retn_shift, recv_shift)), (second, retn_shift))
            ):
                far = index >= LOCAL
                index = index + jnp.where(far, shift, home)
                lane = index & (LANES - 1)
                picks[pl.ds(turn * 8, 4), :] = lane
                picks[pl.ds(turn * 8 + 4, 4), :] = jnp.where(far, BLOCKS, index >> 7)
                codes[turn, four, :] = jnp.where(far, lane + LANES, lane)
            rows_kind[four, :] = kind
            rows_factor[four, :] = jnp.broadcast_to(level_row * float(LIFT * STEP), (4, LANES))
            for face in range(FACES):
                own = range(tree * TREE_BLOCKS, (tree + 1) * TREE_BLOCKS)
                reach = range(BLOCKS) if face == 3 - tree else own
                for turn in range(2):
                    lane = spread(picks[pl.ds(turn * 8 + face, 1), :])
                    place = spread(picks[pl.ds(turn * 8 + 4 + face, 1), :])
                    total = [None] * 4
                    for other in reach:
                        here = place == other
                        for comp in range(4):
                            row = other * TRACE + ((face ^ 1) * 4 + comp) * 8
                            got = pick(traces[pl.ds(row, 8), :], lane)
                            total[comp] = (
                                got if total[comp] is None else jnp.where(here, got, total[comp])
                            )
                    for comp in range(4):
                        row = ((turn * BLOCKS + block) * 4 + face) * 32 + comp * 8
                        found[rows_of(row, 8), :] = total[comp]
            volume_of(state, moved, speeds, base, into, spread(level_row))
            return carry

        lax.fori_loop(0, TREE_BLOCKS, body, 0)


def numeric_flux(left, right, quarter):
    inv_l, inv_r = 1.0 / left[0], 1.0 / right[0]
    un_l, un_r = left[1] * inv_l, right[1] * inv_r
    un = un_l + un_r
    ut = left[2] * inv_l + right[2] * inv_r
    half = 0.5 * jnp.maximum(
        jnp.abs(un_l) + left[0] * lax.rsqrt(left[0]), jnp.abs(un_r) + right[0] * lax.rsqrt(right[0])
    )
    first = (quarter * (left[0] + right[0])) * un
    middle = 0.5 * first
    second = middle * un + quarter * (left[0] * left[0] + right[0] * right[0])
    third = middle * ut
    return (
        first - half * ((right[0] + right[3]) - (left[0] + left[3])),
        second - half * (right[1] - left[1]),
        third - half * (right[2] - left[2]),
    )


def weighted(coefficients, values):
    total = None
    for coefficient, value in zip(coefficients, values):
        term = float(coefficient) * value
        total = term if total is None else total + term
    return total


def surface_kernel(
    moved_in, traces, found, codes, rows_kind, rows_factor, got_wa, got_nb, got_na, got_wb,
    new_depth, new_moment, moved, came, near, changes, sems
):
    del moved_in
    wide_even = (lax.axis_index("wide") & 1) == 0
    narrow_even = (lax.axis_index("narrow") & 1) == 0
    for comp in range(4):
        rows = pl.ds(comp * 8, 8)
        wide = got_wa[rows, :], got_wb[rows, :]
        narrow = got_na[rows, :], got_nb[rows, :]
        came[pl.ds(comp * 8, 8), :] = jnp.where(wide_even, wide[1], wide[0])
        came[pl.ds(32 + comp * 8, 8), :] = jnp.where(wide_even, wide[0], wide[1])
        came[pl.ds(64 + comp * 8, 8), :] = jnp.where(narrow_even, narrow[1], narrow[0])
        came[pl.ds(96 + comp * 8, 8), :] = jnp.where(narrow_even, narrow[0], narrow[1])
    row_id = lax.broadcasted_iota(I32, (8, LANES), 0)
    quarter = jnp.where((row_id & 1) == 1, 0.25, -0.25).astype(F32)

    def copies(block):
        lanes = lanes_of(block)
        row = pl.multiple_of(block * MOVED, MOVED)
        return (
            pltpu.make_async_copy(moved.at[pl.ds(row, 64)], new_depth.at[:, lanes], sems.at[0, block]),
            pltpu.make_async_copy(
                moved.at[pl.ds(row + 64, 128)], new_moment.at[:, lanes], sems.at[1, block]
            ),
        )

    def body(group, carry):
        for face in range(FACES):
            for turn in range(2):
                for half in range(2):
                    spot = half * 4 + face
                    code = spread(codes[turn, pl.ds(group * 8 + spot, 1), :])
                    far = code >= LANES
                    lane = code & (LANES - 1)
                    for comp in range(4):
                        row = ((turn * BLOCKS + group * 2 + half) * 4 + face) * 32 + comp * 8
                        there = pick(came[pl.ds(face * 32 + comp * 8, 8), :], lane)
                        near[pl.ds((turn * 4 + comp) * 64 + spot * 8, 8), :] = jnp.where(
                            far, there, found[rows_of(row, 8), :]
                        )
        eight = pl.ds(pl.multiple_of(group * 8, 8), 8)
        kind = rows_kind[eight, :]
        factor = rows_factor[eight, :]
        coarse, lower, upper = kind == 3, kind == 1, kind == 2
        left, right, high = [], [], []
        for comp in range(4):
            own = [
                traces[pl.ds(group * 256 + comp * 8 + node, 8, stride=32), :] for node in range(8)
            ]
            other = [near[pl.ds(comp * 64 + node, 8, stride=8), :] for node in range(8)]
            blend = [jnp.where(coarse, own[n], other[n]) for n in range(8)]
            even = [blend[b] + blend[7 - b] for b in range(4)]
            odd = [blend[b] - blend[7 - b] for b in range(4)]
            low_of, high_of = [None] * 8, [None] * 8
            for a in range(8):
                one, two = weighted(FOLD_EVEN[a], even), weighted(FOLD_ODD[a], odd)
                low_of[a] = one + two
                high_of[7 - a] = one - two
            left.append([jnp.where(coarse, low_of[n], own[n]) for n in range(8)])
            right.append(
                [jnp.where(lower, low_of[n], jnp.where(upper, high_of[n], other[n])) for n in range(8)]
            )
            high.append(high_of)
        one, two = [], []
        for node in range(8):
            above = [near[pl.ds((4 + comp) * 64 + node, 8, stride=8), :] for comp in range(4)]
            one.append(numeric_flux([v[node] for v in left], [v[node] for v in right], quarter))
            two.append(numeric_flux([v[node] for v in high], above, quarter))
        for comp in range(3):
            total = [one[b][comp] + two[7 - b][comp] for b in range(8)]
            differ = [one[b][comp] - two[7 - b][comp] for b in range(8)]
            for a in range(4):
                same, anti = weighted(JOIN_SUM[a], total), weighted(JOIN_DIFF[a], differ)
                for node, joined in ((a, same + anti), (7 - a, same - anti)):
                    changes[pl.ds(comp * 64 + node, 8, stride=8), :] = factor * jnp.where(
                        coarse, joined, one[node][comp]
                    )
        for half in range(2):
            into = pl.multiple_of((group * 2 + half) * MOVED, MOVED)
            for face in range(FACES):
                for comp in range(3):
                    rows = face_rows(into + component(face, comp) * 64, face)
                    moved[rows, :] = (
                        moved[rows, :] - changes[pl.ds(comp * 64 + (half * 4 + face) * 8, 8), :]
                    )
            for copy in copies(group * 2 + half):
                copy.start()
        return carry

    lax.fori_loop(0, GROUPS, body, 0)

    def finish(block, carry):
        for copy in copies(block):
            copy.wait()
        return carry

    lax.fori_loop(0, BLOCKS, finish, 0)


VM = pl.BlockSpec(memory_space=pltpu.VMEM)
FAR = pl.BlockSpec(memory_space=pltpu.HBM)
ANY = pl.BlockSpec(memory_space=pl.ANY)
PARAMS = pltpu.CompilerParams(vmem_limit_bytes=24 * 1024 * 1024)


def swap(block, axis, phase):
    size = lax.axis_size(axis)
    route = [(i, (((i + phase) ^ 1) - phase) % size) for i in range(size)]
    return lax.ppermute(block, axis, route)


def placed(memory, *arrays):
    return [pltpu.with_memory_space_constraint(array, memory) for array in arrays]


def on_device(depth, momentum, bed, levels, kinds, send, trace_src, back, mortar_src):
    depth = depth.reshape(64, ELEMS)
    momentum = momentum.reshape(128, ELEMS)
    bed = bed.reshape(64, ELEMS)
    message = pltpu.VMEM((32, LANES), F32)
    state, traces, wide_a, narrow_b, narrow_a, wide_b = pl.pallas_call(
        pack_kernel,
        out_shape=(
            pltpu.VMEM((BLOCKS * STATE, LANES), F32),
            pltpu.VMEM((BLOCKS * TRACE, LANES), F32),
            message,
            message,
            message,
            message,
        ),
        in_specs=[FAR] * 5,
        out_specs=[VM] * 6,
        scratch_shapes=[
            pltpu.VMEM((144,), I32),
            pltpu.VMEM((96,), I32),
            pltpu.SemaphoreType.DMA((3, BLOCKS)),
            pltpu.SemaphoreType.DMA((2,)),
        ],
        compiler_params=PARAMS,
        name="pack",
    )(*placed(pltpu.HBM, depth, momentum, bed, send, back))
    got_wb = swap(wide_b, "wide", 1)
    got_na = swap(narrow_a, "narrow", 0)
    got_nb = swap(narrow_b, "narrow", 1)
    got_wa = swap(wide_a, "wide", 0)
    moved, found, codes, rows_kind, rows_factor = pl.pallas_call(
        interior_kernel,
        out_shape=(
            pltpu.VMEM((BLOCKS * MOVED, LANES), F32),
            pltpu.VMEM((2 * BLOCKS * 128, LANES), F32),
            pltpu.VMEM((2, 4 * BLOCKS, LANES), I32),
            pltpu.VMEM((4 * BLOCKS, LANES), I32),
            pltpu.VMEM((4 * BLOCKS, LANES), F32),
        ),
        in_specs=[VM] * 6,
        out_specs=[VM] * 5,
        scratch_shapes=[pltpu.VMEM((128, LANES), F32), pltpu.VMEM((16, LANES), I32)],
        compiler_params=PARAMS,
        name="interior",
        cost_estimate=pl.CostEstimate(flops=20_000_000, bytes_accessed=2_000_000, transcendentals=0),
    )(*placed(pltpu.VMEM, state, traces, kinds, trace_src, mortar_src, levels))
    new_depth, new_moment, _ = pl.pallas_call(
        surface_kernel,
        out_shape=(
            jax.ShapeDtypeStruct((64, ELEMS), F32),
            jax.ShapeDtypeStruct((128, ELEMS), F32),
            pltpu.VMEM((BLOCKS * MOVED, LANES), F32),
        ),
        in_specs=[VM] * 10,
        out_specs=[ANY, ANY, VM],
        input_output_aliases={0: 2},
        scratch_shapes=[
            pltpu.VMEM((128, LANES), F32),
            pltpu.VMEM((512, LANES), F32),
            pltpu.VMEM((192, LANES), F32),
            pltpu.SemaphoreType.DMA((2, BLOCKS)),
        ],
        compiler_params=PARAMS,
        name="surface",
    )(
        *placed(
            pltpu.VMEM, moved, traces, found, codes, rows_kind, rows_factor, got_wa, got_nb, got_na, got_wb
        )
    )
    return new_depth.reshape(8, 8, ELEMS), new_moment.reshape(2, 8, 8, ELEMS)


def solution(mesh):
    both = ("wide", "narrow")
    placed = (
        P(None, None, both),
        P(None, None, None, both),
        P(None, None, both),
        P(both),
        P(None, both),
        P(both),
        P(None, both),
        P(both),
        P(None, None, both),
    )
    return jax.shard_map(
        on_device,
        mesh=mesh,
        in_specs=placed,
        out_specs=(P(None, None, both), P(None, None, None, both)),
        check_vma=False,
    )
```

time: 33 us -> 21 us (0.64)
  Pallas kernels: 17.4 us -> 10.7 us
  local copies, waits for them, and re-layouts: 4.26 us -> 0.02 us
  starting transfers between devices: 10.3 us -> 9.25 us
    pallas_call x1, Pallas kernels: 9.54 us -> 3.28 us  [on_device(): pl.pallas_call(surface_kernel, out_shape=(jax.ShapeDtypeStruct((64, ELEMS...]
    reshape x3 -> x0, local copies, waits for them, and re-layouts: 2.4 us -> none  [the longest x1 1.19 us: on_device(): back = jnp.pad(back, (0, 32)).reshape(1, 128)]
    pad x1 -> x0, local copies, waits for them, and re-layouts: 1.26 us -> none  [on_device(): send = jnp.pad(send, (0, 112)).reshape(1, 256)]
    ppermute x4, starting transfers between devices: 10.3 us -> 9.25 us  [swap(): return lax.ppermute(block, axis, route)]
    unnamed x12 -> x8, local copies, waits for them, and re-layouts: 0.6 us -> 0.02 us
    pallas_call x2, Pallas kernels: 7.87 us -> 7.42 us  [the longest x1 4.91 us: on_device(): pl.pallas_call(interior_kernel, out_shape=(pltpu.VMEM((BLOCKS * MOVED, LA...]
  transfers between devices with their start and end apart: 4 -> 4, of which waited for: 0 -> 0; matrix products, arithmetic and copies ran while one was open for 4% -> 0% of each run, Pallas kernels for 13% -> 24%
where the time goes in v2:
time: 21 us; the launch traced here: 20.7 us
  Pallas kernels  10.7 us (51%)
  starting transfers between devices  9.25 us (44%)
  between operations  0.72 us (3%)
    ppermute x4, starting transfers between devices, swap(): return lax.ppermute(block, axis, route)  9.25 us
    pallas_call x1, Pallas kernels, on_device(): pl.pallas_call(interior_kernel, out_shape=(pltpu.VMEM((BLOCKS * MOVED, LA...  4.91 us
    pallas_call x1, Pallas kernels, on_device(): pl.pallas_call(surface_kernel, out_shape=(jax.ShapeDtypeStruct((64, ELEMS...  3.28 us
    pallas_call x1, Pallas kernels, on_device(): pl.pallas_call(pack_kernel, out_shape=(pltpu.VMEM((BLOCKS * STATE, LANES)...  2.51 us
  transfers between devices with their start and end apart: 4, of which 0 were waited for; matrix products, arithmetic and copies ran while one was open for 0% of the time, Pallas kernels for 24%

profile of v2, /device:TPU:0, one launch (start us, length us, event | category | flops | bytes accessed | tf_op | source)
XLA Modules:
  0.0 20.7 jit_solution(5855007708514227114)
XLA Ops:
  0.6 0.0 copy-start
  0.6 0.0 copy-start.2
  0.7 0.0 copy-start.1
  0.7 0.0 copy-start.3
  0.7 2.5 %pack.1 = (f32[2560,128]{1,0:T(8,128)S(1)}, f32[1280,128]{1,0:T(8,128)S(1)}, f32[32,128]{1,0:T(8,128)S(1)}, f32[32,128]{1,0:T(8,128)S(1)}, f32[32,128]{1,0:T(8,128)S(1)}, /*index=5*/f32[32,128]{1,0:T(8,128)S(1)}) custom-call(f32[64,1280]{1,0:T(8,128)} %bitcast.6, f32[128,1280]{1,0:T(8,128)} %bitcast.5, f32[64,1280]{1,0:T(8,128)} %bitcast.7, s32[144]{0:T(256)} %send.1, ...), custom_call_target="tpu_custom_call" | custom-call | tf_op jit(solution)/shard_map/pack/pallas_call | solution.py:460
  3.2 0.1 collective-permute-start
  3.3 3.2 %collective-permute-start.1 = (f32[32,128]{1,0:T(8,128)S(1)}, f32[32,128]{1,0:T(8,128)S(1)}, u32[]{:S(2)}, u32[]{:S(2)}) collective-permute-start(f32[32,128]{1,0:T(8,128)S(1)} %get-tuple-element.23), channel_id=1, source_target_pairs={{0,3},{1,2},{2,1},{3,0},{4,7},{5,6},{6,5},{7,4},{8,11},{9,10},{10,... | collective-permute-start | bytes 49160 | tf_op jit(solution)/shard_map/ppermute | solution.py:448
  6.5 0.1 collective-permute-start.2
  6.6 5.9 %collective-permute-start.3 = (f32[32,128]{1,0:T(8,128)S(1)}, f32[32,128]{1,0:T(8,128)S(1)}, u32[]{:S(2)}, u32[]{:S(2)}) collective-permute-start(f32[32,128]{1,0:T(8,128)S(1)} %get-tuple-element.25), channel_id=1, source_target_pairs={{0,124},{4,8},{8,4},{12,16},{16,12},{20,24},{24,20},{28,32},{32,28... | collective-permute-start | bytes 49160 | tf_op jit(solution)/shard_map/ppermute | solution.py:448
  12.5 0.0 copy-done
  12.5 0.0 copy-done.2
  12.5 0.0 copy-done.1
  12.5 0.0 copy-done.3
  12.5 4.9 %interior.1 = (f32[1920,128]{1,0:T(8,128)S(1)}, f32[2560,128]{1,0:T(8,128)S(1)}, s32[2,40,128]{2,1,0:T(8,128)S(1)}, s32[40,128]{1,0:T(8,128)S(1)}, f32[40,128]{1,0:T(8,128)S(1)}) custom-call(f32[2560,128]{1,0:T(8,128)S(1)} %get-tuple-element.15.state, f32[1280,128]{1,0:T(8,128)S(1)} %get-tuple-element.16.traces, s32[4,1280]{1,0:T(4,128)S(1)} %copy-done.1, ...), custom_call_target="tpu_custom_call" | custom-call | flops 20000000 | bytes 2000000 | tf_op jit(solution)/shard_map/interior/pallas_call | solution.py:485
  17.4 0.0 collective-permute-done.got_wa
  17.4 0.0 collective-permute-done.1.got_nb
  17.4 0.0 collective-permute-done.2.got_na
  17.4 0.0 collective-permute-done.3.got_wb
  17.4 3.3 %surface.1 = (f32[64,1280]{1,0:T(8,128)}, f32[128,1280]{1,0:T(8,128)}, f32[1920,128]{1,0:T(8,128)S(1)}) custom-call(f32[1920,128]{1,0:T(8,128)S(1)} %get-tuple-element.17.moved_in, f32[1280,128]{1,0:T(8,128)S(1)} %get-tuple-element.16.traces, f32[2560,128]{1,0:T(8,128)S(1)} %get-tuple-element.18.found, ...), custom_call_target="tpu_custom_call", output_to_operand_aliasing={{2}: (0, {})} | custom-call | tf_op jit(solution)/shard_map/surface/pallas_call | solution.py:501
Async XLA Ops:
  0.6 11.8 %copy-start = (s32[2,4,1280]{2,1,0:T(4,128)S(1)}, s32[2,4,1280]{2,1,0:T(4,128)}, u32[]{:S(2)}) copy-start(s32[2,4,1280]{2,1,0:T(4,128)} %mortar_src.1) | copy-start | bytes 122884
  0.6 11.8 %copy-start.2 = (s32[4,1280]{1,0:T(4,128)S(1)}, s32[4,1280]{1,0:T(4,128)}, u32[]{:S(2)}) copy-start(s32[4,1280]{1,0:T(4,128)} %trace_src.1) | copy-start | bytes 61444
  0.7 11.8 %copy-start.1 = (s32[4,1280]{1,0:T(4,128)S(1)}, s32[4,1280]{1,0:T(4,128)}, u32[]{:S(2)}) copy-start(s32[4,1280]{1,0:T(4,128)} %kinds.1) | copy-start | bytes 61444
  0.7 11.8 %copy-start.3 = (s32[1280]{0:T(1024)S(1)}, s32[1280]{0:T(1024)}, u32[]{:S(2)}) copy-start(s32[1280]{0:T(1024)} %levels.1) | copy-start | bytes 15364
  3.2 14.2 %collective-permute-start = (f32[32,128]{1,0:T(8,128)S(1)}, f32[32,128]{1,0:T(8,128)S(1)}, u32[]{:S(2)}, u32[]{:S(2)}) collective-permute-start(f32[32,128]{1,0:T(8,128)S(1)} %get-tuple-element.22), channel_id=1, source_target_pairs={{0,4},{4,0},{8,12},{12,8},{16,20},{20,16},{24,28},{28,24},{32,36},... | collective-permute-start | bytes 49160 | tf_op jit(solution)/shard_map/ppermute | solution.py:448
  3.3 14.1 %collective-permute-start.1 = (f32[32,128]{1,0:T(8,128)S(1)}, f32[32,128]{1,0:T(8,128)S(1)}, u32[]{:S(2)}, u32[]{:S(2)}) collective-permute-start(f32[32,128]{1,0:T(8,128)S(1)} %get-tuple-element.23), channel_id=1, source_target_pairs={{0,3},{1,2},{2,1},{3,0},{4,7},{5,6},{6,5},{7,4},{8,11},{9,10},{10,... | collective-permute-start | bytes 49160 | tf_op jit(solution)/shard_map/ppermute | solution.py:448
  6.5 10.9 %collective-permute-start.2 = (f32[32,128]{1,0:T(8,128)S(1)}, f32[32,128]{1,0:T(8,128)S(1)}, u32[]{:S(2)}, u32[]{:S(2)}) collective-permute-start(f32[32,128]{1,0:T(8,128)S(1)} %get-tuple-element.24), channel_id=1, source_target_pairs={{0,1},{1,0},{2,3},{3,2},{4,5},{5,4},{6,7},{7,6},{8,9},{9,8},{10,11... | collective-permute-start | bytes 49160 | tf_op jit(solution)/shard_map/ppermute | solution.py:448
  6.6 10.8 %collective-permute-start.3 = (f32[32,128]{1,0:T(8,128)S(1)}, f32[32,128]{1,0:T(8,128)S(1)}, u32[]{:S(2)}, u32[]{:S(2)}) collective-permute-start(f32[32,128]{1,0:T(8,128)S(1)} %get-tuple-element.25), channel_id=1, source_target_pairs={{0,124},{4,8},{8,4},{12,16},{16,12},{20,24},{24,20},{28,32},{32,28... | collective-permute-start | bytes 49160 | tf_op jit(solution)/shard_map/ppermute | solution.py:448

commit v3 on v2

--- a/solution.py
+++ b/solution.py
@@ -9,6 +9,7 @@
 NODES = 8
 ELEMS = 1280
 LANES = 128
+AHEAD = 35
 BLOCKS = ELEMS // LANES
 TREE_BLOCKS = BLOCKS // 2
 GROUPS = BLOCKS // 2
@@ -110,9 +111,12 @@
 
 
 def pack_kernel(
-    depth, moment, bed, send, back, state, traces, wide_a, narrow_b, narrow_a, wide_b,
-    send_list, back_list, sems, list_sems
+    depth, moment, bed, send, back, kinds_far, trace_far, mortar_far, levels_far,
+    state, traces, wide_a, narrow_b, narrow_a, wide_b, kinds, trace_src, mortar_src, levels,
+    *rest
 ):
+    out_refs, scratch = rest[:5], rest[5:7]
+    send_list, back_list, sems, list_sems = rest[7:]
     list_copies = [
         pltpu.make_async_copy(send, send_list, list_sems.at[0]),
         pltpu.make_async_copy(back, back_list, list_sems.at[1]),
@@ -120,6 +124,12 @@
     for copy in list_copies:
         copy.start()
     copies = []
+    table_copies = [
+        pltpu.make_async_copy(kinds_far, kinds, list_sems.at[2]),
+        pltpu.make_async_copy(trace_far, trace_src, list_sems.at[3]),
+        pltpu.make_async_copy(mortar_far, mortar_src, list_sems.at[4]),
+        pltpu.make_async_copy(levels_far, levels, list_sems.at[5]),
+    ]
     for block in range(BLOCKS):
         lanes = pl.ds(block * LANES, LANES)
         base = block * STATE
@@ -131,6 +141,8 @@
             )
             copy.start()
             copies.append(copy)
+    for copy in table_copies:
+        copy.start()
     for copy in list_copies:
         copy.wait()
     lane_id = lax.broadcasted_iota(I32, (8, LANES), 1)
@@ -156,12 +168,17 @@
     for block in range(BLOCKS):
         for copy in copies[3 * block : 3 * block + 3]:
             copy.wait()
-        for way in range(4):
+        for face in range(FACES):
+            for comp in range(4):
+                traces[pl.ds(block * TRACE + (face * 4 + comp) * 8, 8), :] = state[
+                    face_rows(block * STATE + component(face, comp) * 64, face), :
+                ]
+    for way in range(4):
+        for block in range(BLOCKS):
             here = place[way] == block
             for comp in range(4):
-                piece = state[face_rows(block * STATE + component(way, comp) * 64, way), :]
-                traces[pl.ds(block * TRACE + (way * 4 + comp) * 8, 8), :] = piece
-                out[way][comp] = jnp.where(here, pick(piece, lane[way]), out[way][comp])
+                got = pick(traces[pl.ds(block * TRACE + (way * 4 + comp) * 8, 8), :], lane[way])
+                out[way][comp] = got if block == 0 else jnp.where(here, got, out[way][comp])
     wide_even = (lax.axis_index("wide") & 1) == 0
     narrow_even = (lax.axis_index("narrow") & 1) == 0
     for comp in range(4):
@@ -170,6 +187,15 @@
         wide_b[rows, :] = jnp.where(wide_even, out[0][comp], out[1][comp])
         narrow_a[rows, :] = jnp.where(narrow_even, out[3][comp], out[2][comp])
         narrow_b[rows, :] = jnp.where(narrow_even, out[2][comp], out[3][comp])
+    for copy in table_copies:
+        copy.wait()
+    work = block_worker(state, traces, kinds, trace_src, mortar_src, levels, out_refs, scratch)
+
+    def first_tree(block, carry):
+        work(block, 0)
+        return carry
+
+    lax.fori_loop(0, blocks_ahead(), first_tree, 0)
 
 
 def line_terms(height, normal, tangent, bed):
@@ -185,6 +211,7 @@
             bump = float(SKEW[i, k]) * (bed[k] - bed[i])
             accumulate(slope, i, bump)
             accumulate(slope, k, bump)
+        yield
     square = [2.0 * (h * h) for h in height]
     mass = [None] * 8
     along = [(4.0 * height[i]) * slope[i] for i in range(8)]
@@ -199,6 +226,7 @@
             for slot, value in ((mass, first), (along, second), (cross, third)):
                 accumulate(slot, i, value)
                 accumulate(slot, k, value, True)
+            yield
     out = []
     for i in range(8):
         scale = STEP / WEIGHTS[i]
@@ -226,7 +254,7 @@
         vel_y.append(state[at(base, rows(2, j, False)), :] * inverse)
         speeds[rows(0, j, False), :] = vel_x[j]
         speeds[rows(1, j, False), :] = vel_y[j]
-    terms = line_terms(height, vel_x, vel_y, bed)
+    terms = yield from line_terms(height, vel_x, vel_y, bed)
     for i in range(8):
         for comp, value in enumerate(terms[i]):
             moved[at(into, rows(comp, i, False)), :] = (
@@ -236,7 +264,7 @@
     bed = [state[at(base, rows(3, j, True)), :] for j in range(8)]
     vel_x = [speeds[rows(0, j, True), :] for j in range(8)]
     vel_y = [speeds[rows(1, j, True), :] for j in range(8)]
-    terms = line_terms(height, vel_y, vel_x, bed)
+    terms = yield from line_terms(height, vel_y, vel_x, bed)
     for j in range(8):
         mass, along, cross = terms[j]
         for comp, value in enumerate((mass, cross, along)):
@@ -244,10 +272,37 @@
             moved[window, :] = moved[window, :] - metric * value
 
 
-def interior_kernel(
-    state, traces, kinds, trace_src, mortar_src, levels, moved, found, codes, rows_kind, rows_factor,
-    speeds, picks
-):
+def gather_of(traces, found, picks, block, tree):
+    for face in range(FACES):
+        own = range(tree * TREE_BLOCKS, (tree + 1) * TREE_BLOCKS)
+        reach = range(BLOCKS) if face == 3 - tree else own
+        for turn in range(2):
+            lane = spread(picks[pl.ds(turn * 8 + face, 1), :])
+            place = spread(picks[pl.ds(turn * 8 + 4 + face, 1), :])
+            total = [None] * 4
+            for other in reach:
+                here = place == other
+                for comp in range(4):
+                    row = other * TRACE + ((face ^ 1) * 4 + comp) * 8
+                    got = pick(traces[pl.ds(row, 8), :], lane)
+                    total[comp] = got if total[comp] is None else jnp.where(here, got, total[comp])
+                yield
+            for comp in range(4):
+                row = ((turn * BLOCKS + block) * 4 + face) * 32 + comp * 8
+                found[rows_of(row, 8), :] = total[comp]
+
+
+def interleave(*works):
+    works = list(works)
+    while works:
+        for work in list(works):
+            if next(work, works) is works:
+                works.remove(work)
+
+
+def block_worker(state, traces, kinds, trace_src, mortar_src, levels, out, scratch):
+    moved, found, codes, rows_kind, rows_factor = out
+    speeds, picks = scratch
     face_id = lax.broadcasted_iota(I32, (4, LANES), 0)
 
     def by_face(values):
@@ -260,52 +315,65 @@
     recv_shift = by_face([RECV_LANE[f] - RECV_OFF[f] - LOCAL for f in range(FACES)])
     retn_shift = by_face([RETN_LANE[f] - RETN_OFF[f] - LOCAL for f in range(FACES)])
 
-    for tree in range(2):
-
-        def body(step, carry, tree=tree):
-            block = step + tree * TREE_BLOCKS
-            lanes = lanes_of(block)
-            base = pl.multiple_of(block * STATE, STATE)
-            into = pl.multiple_of(block * MOVED, MOVED)
-            level_row = (levels[lanes].reshape(1, LANES) + 1).astype(F32)
-            kind = kinds[:, lanes]
-            coarse = kind == 3
-            first = jnp.where(coarse, mortar_src[0, :, lanes], trace_src[:, lanes])
-            second = mortar_src[1, :, lanes]
-            four = pl.ds(pl.multiple_of(block * 4, 4), 4)
-            for turn, (index, shift) in enumerate(
-                ((first, jnp.where(coarse, retn_shift, recv_shift)), (second, retn_shift))
-            ):
-                far = index >= LOCAL
-                index = index + jnp.where(far, shift, home)
-                lane = index & (LANES - 1)
-                picks[pl.ds(turn * 8, 4), :] = lane
-                picks[pl.ds(turn * 8 + 4, 4), :] = jnp.where(far, BLOCKS, index >> 7)
-                codes[turn, four, :] = jnp.where(far, lane + LANES, lane)
-            rows_kind[four, :] = kind
-            rows_factor[four, :] = jnp.broadcast_to(level_row * float(LIFT * STEP), (4, LANES))
-            for face in range(FACES):
-                own = range(tree * TREE_BLOCKS, (tree + 1) * TREE_BLOCKS)
-                reach = range(BLOCKS) if face == 3 - tree else own
-                for turn in range(2):
-                    lane = spread(picks[pl.ds(turn * 8 + face, 1), :])
-                    place = spread(picks[pl.ds(turn * 8 + 4 + face, 1), :])
-                    total = [None] * 4
-                    for other in reach:
-                        here = place == other
-                        for comp in range(4):
-                            row = other * TRACE + ((face ^ 1) * 4 + comp) * 8
-                            got = pick(traces[pl.ds(row, 8), :], lane)
-                            total[comp] = (
-                                got if total[comp] is None else jnp.where(here, got, total[comp])
-                            )
-                    for comp in range(4):
-                        row = ((turn * BLOCKS + block) * 4 + face) * 32 + comp * 8
-                        found[rows_of(row, 8), :] = total[comp]
-            volume_of(state, moved, speeds, base, into, spread(level_row))
-            return carry
-
-        lax.fori_loop(0, TREE_BLOCKS, body, 0)
+    def work(block, tree):
+        lanes = lanes_of(block)
+        base = pl.multiple_of(block * STATE, STATE)
+        into = pl.multiple_of(block * MOVED, MOVED)
+        level_row = (levels[lanes].reshape(1, LANES) + 1).astype(F32)
+        kind = kinds[:, lanes]
+        coarse = kind == 3
+        first = jnp.where(coarse, mortar_src[0, :, lanes], trace_src[:, lanes])
+        second = mortar_src[1, :, lanes]
+        four = pl.ds(pl.multiple_of(block * 4, 4), 4)
+        for turn, (index, shift) in enumerate(
+            ((first, jnp.where(coarse, retn_shift, recv_shift)), (second, retn_shift))
+        ):
+            far = index >= LOCAL
+            index = index + jnp.where(far, shift, home)
+            lane = index & (LANES - 1)
+            picks[pl.ds(turn * 8, 4), :] = lane
+            picks[pl.ds(turn * 8 + 4, 4), :] = jnp.where(far, BLOCKS, index >> 7)
+            codes[turn, four, :] = jnp.where(far, lane + LANES, lane)
+        rows_kind[four, :] = kind
+        rows_factor[four, :] = jnp.broadcast_to(level_row * float(LIFT * STEP), (4, LANES))
+        interleave(
+            volume_of(state, moved, speeds, base, into, spread(level_row)),
+            gather_of(traces, found, picks, block, tree),
+        )
+
+    return work
+
+
+def blocks_ahead():
+    wide, narrow = lax.axis_index("wide"), lax.axis_index("narrow")
+    x, z, core = wide >> 3, (wide >> 1) & 3, wide & 1
+
+    def one_of(at, values):
+        total = jnp.int32(values[3])
+        for i in range(3):
+            total = jnp.where(at == i, jnp.int32(values[i]), total)
+        return total
+
+    lead = AHEAD - one_of(narrow, (0, 7, 15, 19)) - one_of(x, (0, 10, 12, 14)) - one_of(z, (0, 10, 22, 26))
+    return jnp.clip((lead + 5 * core) // 5, 0, TREE_BLOCKS)
+
+
+def interior_kernel(
+    state, traces, kinds, trace_src, mortar_src, levels, *rest
+):
+    out, scratch = rest[5:10], rest[10:]
+    work = block_worker(state, traces, kinds, trace_src, mortar_src, levels, out, scratch)
+
+    def first_tree(block, carry):
+        work(block, 0)
+        return carry
+
+    def second_tree(block, carry):
+        work(block, 1)
+        return carry
+
+    lax.fori_loop(blocks_ahead(), TREE_BLOCKS, first_tree, 0)
+    lax.fori_loop(TREE_BLOCKS, BLOCKS, second_tree, 0)
 
 
 def numeric_flux(left, right, quarter):
@@ -457,47 +525,53 @@
     momentum = momentum.reshape(128, ELEMS)
     bed = bed.reshape(64, ELEMS)
     message = pltpu.VMEM((32, LANES), F32)
-    state, traces, wide_a, narrow_b, narrow_a, wide_b = pl.pallas_call(
+    tables = (
+        pltpu.VMEM((4, ELEMS), I32),
+        pltpu.VMEM((4, ELEMS), I32),
+        pltpu.VMEM((2, 4, ELEMS), I32),
+        pltpu.VMEM((ELEMS,), I32),
+    )
+    done = (
+        pltpu.VMEM((BLOCKS * MOVED, LANES), F32),
+        pltpu.VMEM((2 * BLOCKS * 128, LANES), F32),
+        pltpu.VMEM((2, 4 * BLOCKS, LANES), I32),
+        pltpu.VMEM((4 * BLOCKS, LANES), I32),
+        pltpu.VMEM((4 * BLOCKS, LANES), F32),
+    )
+    held = pltpu.VMEM((BLOCKS * STATE, LANES), F32), pltpu.VMEM((BLOCKS * TRACE, LANES), F32)
+    work_space = [pltpu.VMEM((128, LANES), F32), pltpu.VMEM((16, LANES), I32)]
+    packed = pl.pallas_call(
         pack_kernel,
-        out_shape=(
-            pltpu.VMEM((BLOCKS * STATE, LANES), F32),
-            pltpu.VMEM((BLOCKS * TRACE, LANES), F32),
-            message,
-            message,
-            message,
-            message,
-        ),
-        in_specs=[FAR] * 5,
-        out_specs=[VM] * 6,
-        scratch_shapes=[
+        out_shape=held + (message,) * 4 + tables + done,
+        in_specs=[FAR] * 9,
+        out_specs=[VM] * 15,
+        scratch_shapes=work_space
+        + [
             pltpu.VMEM((144,), I32),
             pltpu.VMEM((96,), I32),
             pltpu.SemaphoreType.DMA((3, BLOCKS)),
-            pltpu.SemaphoreType.DMA((2,)),
+            pltpu.SemaphoreType.DMA((6,)),
         ],
         compiler_params=PARAMS,
         name="pack",
-    )(*placed(pltpu.HBM, depth, momentum, bed, send, back))
+    )(*placed(pltpu.HBM, depth, momentum, bed, send, back, kinds, trace_src, mortar_src, levels))
+    state, traces = packed[:2]
+    wide_a, narrow_b, narrow_a, wide_b = packed[2:6]
     got_wb = swap(wide_b, "wide", 1)
     got_na = swap(narrow_a, "narrow", 0)
     got_nb = swap(narrow_b, "narrow", 1)
     got_wa = swap(wide_a, "wide", 0)
     moved, found, codes, rows_kind, rows_factor = pl.pallas_call(
         interior_kernel,
-        out_shape=(
-            pltpu.VMEM((BLOCKS * MOVED, LANES), F32),
-            pltpu.VMEM((2 * BLOCKS * 128, LANES), F32),
-            pltpu.VMEM((2, 4 * BLOCKS, LANES), I32),
-            pltpu.VMEM((4 * BLOCKS, LANES), I32),
-            pltpu.VMEM((4 * BLOCKS, LANES), F32),
-        ),
-        in_specs=[VM] * 6,
+        out_shape=done,
+        in_specs=[VM] * 11,
         out_specs=[VM] * 5,
-        scratch_shapes=[pltpu.VMEM((128, LANES), F32), pltpu.VMEM((16, LANES), I32)],
+        input_output_aliases={6 + i: i for i in range(5)},
+        scratch_shapes=work_space,
         compiler_params=PARAMS,
         name="interior",
         cost_estimate=pl.CostEstimate(flops=20_000_000, bytes_accessed=2_000_000, transcendentals=0),
-    )(*placed(pltpu.VMEM, state, traces, kinds, trace_src, mortar_src, levels))
+    )(*placed(pltpu.VMEM, state, traces, *packed[6:15]))
     new_depth, new_moment, _ = pl.pallas_call(
         surface_kernel,
         out_shape=(

time: 21 us -> 18.1 us (0.86)
  starting transfers between devices: 9.25 us -> 6.8 us
  Pallas kernels: 10.7 us -> 10.1 us
  waiting for transfers between devices: 0.01 us -> 0.36 us
    ppermute x4, starting transfers between devices: 9.25 us -> 6.8 us  [swap(): return lax.ppermute(block, axis, route)]
    pallas_call x2, Pallas kernels: 7.42 us -> 6.84 us  [the longest x1 4.41 us: on_device(): pl.pallas_call(pack_kernel, out_shape=held + (message,) * 4 + tables + do...]
    ppermute x4, waiting for transfers between devices: 0.01 us -> 0.36 us  [swap(): return lax.ppermute(block, axis, route)]
  transfers between devices with their start and end apart: 4 -> 4, of which waited for: 0 -> 1; matrix products, arithmetic and copies ran while one was open for 0% -> 0% of each run, Pallas kernels for 24% -> 14%
where the time goes in v3:
time: 18.1 us; the launch traced here: 18 us
  Pallas kernels  10.1 us (56%)
  starting transfers between devices  6.8 us (38%)
  between operations  0.68 us (4%)
  waiting for transfers between devices  0.36 us (2%)
    ppermute x4, starting transfers between devices, swap(): return lax.ppermute(block, axis, route)  6.8 us
    pallas_call x1, Pallas kernels, on_device(): pl.pallas_call(pack_kernel, out_shape=held + (message,) * 4 + tables + do...  4.41 us
    pallas_call x1, Pallas kernels, on_device(): pl.pallas_call(surface_kernel, out_shape=(jax.ShapeDtypeStruct((64, ELEMS...  3.28 us
    pallas_call x1, Pallas kernels, on_device(): pl.pallas_call(interior_kernel, out_shape=done, in_specs=[VM] * 11, out_s...  2.44 us
    ppermute x4, waiting for transfers between devices, swap(): return lax.ppermute(block, axis, route)  0.36 us
  transfers between devices with their start and end apart: 4, of which 1 were waited for; matrix products, arithmetic and copies ran while one was open for 0% of the time, Pallas kernels for 14%

profile of v3, /device:TPU:0, one launch (start us, length us, event | category | flops | bytes accessed | tf_op | source)
XLA Modules:
  0.0 18.0 jit_solution(7670704105369983798)
XLA Ops:
  0.6 4.4 %pack.1 = (f32[2560,128]{1,0:T(8,128)S(1)}, f32[1280,128]{1,0:T(8,128)S(1)}, f32[32,128]{1,0:T(8,128)S(1)}, f32[32,128]{1,0:T(8,128)S(1)}, f32[32,128]{1,0:T(8,1...) custom-call(f32[64,1280]{1,0:T(8,128)} %bitcast.6, ...), custom_call_target="tpu_custom_call" | custom-call | tf_op jit(solution)/shard_map/pack/pallas_call | solution.py:543
  5.0 0.1 collective-permute-start
  5.1 2.4 %collective-permute-start.1 = (f32[32,128]{1,0:T(8,128)S(1)}, f32[32,128]{1,0:T(8,128)S(1)}, u32[]{:S(2)}, u32[]{:S(2)}) collective-permute-start(f32[32,128]{1,0:T(8,128)S(1)} %get-tuple-element.41), channel_id=1, source_target_pairs={{0,3},{1,2},{2,1},{3,0},{4,7},{5,6},{6,5},{7,4},{8,11},{9,10},{10,... | collective-permute-start | bytes 49160 | tf_op jit(solution)/shard_map/ppermute | solution.py:516
  7.6 0.6 %collective-permute-start.2 = (f32[32,128]{1,0:T(8,128)S(1)}, f32[32,128]{1,0:T(8,128)S(1)}, u32[]{:S(2)}, u32[]{:S(2)}) collective-permute-start(f32[32,128]{1,0:T(8,128)S(1)} %get-tuple-element.42), channel_id=1, source_target_pairs={{0,1},{1,0},{2,3},{3,2},{4,5},{5,4},{6,7},{7,6},{8,9},{9,8},{10,11... | collective-permute-start | bytes 49160 | tf_op jit(solution)/shard_map/ppermute | solution.py:516
  8.2 3.7 %collective-permute-start.3 = (f32[32,128]{1,0:T(8,128)S(1)}, f32[32,128]{1,0:T(8,128)S(1)}, u32[]{:S(2)}, u32[]{:S(2)}) collective-permute-start(f32[32,128]{1,0:T(8,128)S(1)} %get-tuple-element.43), channel_id=1, source_target_pairs={{0,124},{4,8},{8,4},{12,16},{16,12},{20,24},{24,20},{28,32},{32,28... | collective-permute-start | bytes 49160 | tf_op jit(solution)/shard_map/ppermute | solution.py:516
  11.9 2.4 %interior.1 = (f32[1920,128]{1,0:T(8,128)S(1)}, f32[2560,128]{1,0:T(8,128)S(1)}, s32[2,40,128]{2,1,0:T(8,128)S(1)}, s32[40,128]{1,0:T(8,128)S(1)}, f32[40,128]{1,0:T(8,128)S(1)}) custom-call(f32[2560,128]{1,0:T(8,128)S(1)} %get-tuple-element.24.state, ...), custom_call_target="tpu_custom_call", output_to_operand_aliasing={{0}: (6, {}), {1}: (7, {}), {2}: (8, {}), {3}: (9, {}), {4}... | custom-call | flops 20000000 | bytes 2000000 | tf_op jit(solution)/shard_map/interior/pallas_call | solution.py:564
  14.3 0.0 collective-permute-done.got_wa
  14.3 0.0 collective-permute-done.1.got_nb
  14.3 0.0 collective-permute-done.2.got_na
  14.3 0.4 %collective-permute-done.3.got_wb = f32[32,128]{1,0:T(8,128)S(1)} collective-permute-done((f32[32,128]{1,0:T(8,128)S(1)}, f32[32,128]{1,0:T(8,128)S(1)}, u32[]{:S(2)}, u32[]{:S(2)}) %collective-permute-start.3) | collective-permute-done | bytes 16416 | tf_op jit(solution)/shard_map/ppermute | solution.py:516
  14.7 3.3 %surface.1 = (f32[64,1280]{1,0:T(8,128)}, f32[128,1280]{1,0:T(8,128)}, f32[1920,128]{1,0:T(8,128)S(1)}) custom-call(f32[1920,128]{1,0:T(8,128)S(1)} %get-tuple-element.35.moved_in, f32[1280,128]{1,0:T(8,128)S(1)} %get-tuple-element.25.traces, f32[2560,128]{1,0:T(8,128)S(1)} %get-tuple-element.36.found, ...), custom_call_target="tpu_custom_call", output_to_operand_aliasing={{2}: (0, {})} | custom-call | tf_op jit(solution)/shard_map/surface/pallas_call | solution.py:575
Async XLA Ops:
  5.0 9.3 %collective-permute-start = (f32[32,128]{1,0:T(8,128)S(1)}, f32[32,128]{1,0:T(8,128)S(1)}, u32[]{:S(2)}, u32[]{:S(2)}) collective-permute-start(f32[32,128]{1,0:T(8,128)S(1)} %get-tuple-element.40), channel_id=1, source_target_pairs={{0,4},{4,0},{8,12},{12,8},{16,20},{20,16},{24,28},{28,24},{32,36},... | collective-permute-start | bytes 49160 | tf_op jit(solution)/shard_map/ppermute | solution.py:516
  5.1 9.2 %collective-permute-start.1 = (f32[32,128]{1,0:T(8,128)S(1)}, f32[32,128]{1,0:T(8,128)S(1)}, u32[]{:S(2)}, u32[]{:S(2)}) collective-permute-start(f32[32,128]{1,0:T(8,128)S(1)} %get-tuple-element.41), channel_id=1, source_target_pairs={{0,3},{1,2},{2,1},{3,0},{4,7},{5,6},{6,5},{7,4},{8,11},{9,10},{10,... | collective-permute-start | bytes 49160 | tf_op jit(solution)/shard_map/ppermute | solution.py:516
  7.6 6.8 %collective-permute-start.2 = (f32[32,128]{1,0:T(8,128)S(1)}, f32[32,128]{1,0:T(8,128)S(1)}, u32[]{:S(2)}, u32[]{:S(2)}) collective-permute-start(f32[32,128]{1,0:T(8,128)S(1)} %get-tuple-element.42), channel_id=1, source_target_pairs={{0,1},{1,0},{2,3},{3,2},{4,5},{5,4},{6,7},{7,6},{8,9},{9,8},{10,11... | collective-permute-start | bytes 49160 | tf_op jit(solution)/shard_map/ppermute | solution.py:516
  8.2 6.5 %collective-permute-start.3 = (f32[32,128]{1,0:T(8,128)S(1)}, f32[32,128]{1,0:T(8,128)S(1)}, u32[]{:S(2)}, u32[]{:S(2)}) collective-permute-start(f32[32,128]{1,0:T(8,128)S(1)} %get-tuple-element.43), channel_id=1, source_target_pairs={{0,124},{4,8},{8,4},{12,16},{16,12},{20,24},{24,20},{28,32},{32,28... | collective-permute-start | bytes 49160 | tf_op jit(solution)/shard_map/ppermute | solution.py:516

commit v4 on v3

--- a/solution.py
+++ b/solution.py
@@ -10,6 +10,7 @@
 ELEMS = 1280
 LANES = 128
 AHEAD = 35
+PER_BLOCK = 5
 BLOCKS = ELEMS // LANES
 TREE_BLOCKS = BLOCKS // 2
 GROUPS = BLOCKS // 2
@@ -198,7 +199,7 @@
     lax.fori_loop(0, blocks_ahead(), first_tree, 0)
 
 
-def line_terms(height, normal, tangent, bed):
+def line_terms(height, normal, tangent, bed, marks):
     def accumulate(slot, i, value, minus=False):
         if slot[i] is None:
             slot[i] = -value if minus else value
@@ -220,6 +221,8 @@
         for k in range(i + 1, 8):
             q = float(SKEW[i, k])
             un = normal[i] + normal[k]
+            if marks:
+                un = un + marks.pop(0)
             first = (q * (height[i] + height[k])) * un
             second = first * un + q * (square[i] + square[k])
             third = first * (tangent[i] + tangent[k])
@@ -236,7 +239,7 @@
     return out
 
 
-def volume_of(state, moved, speeds, base, into, metric):
+def volume_of(state, moved, speeds, base, into, metric, marks):
     def rows(comp, j, across):
         if across:
             return pl.ds(comp * 64 + j, 8, stride=8)
@@ -254,7 +257,7 @@
         vel_y.append(state[at(base, rows(2, j, False)), :] * inverse)
         speeds[rows(0, j, False), :] = vel_x[j]
         speeds[rows(1, j, False), :] = vel_y[j]
-    terms = yield from line_terms(height, vel_x, vel_y, bed)
+    terms = yield from line_terms(height, vel_x, vel_y, bed, marks)
     for i in range(8):
         for comp, value in enumerate(terms[i]):
             moved[at(into, rows(comp, i, False)), :] = (
@@ -264,7 +267,7 @@
     bed = [state[at(base, rows(3, j, True)), :] for j in range(8)]
     vel_x = [speeds[rows(0, j, True), :] for j in range(8)]
     vel_y = [speeds[rows(1, j, True), :] for j in range(8)]
-    terms = yield from line_terms(height, vel_y, vel_x, bed)
+    terms = yield from line_terms(height, vel_y, vel_x, bed, marks)
     for j in range(8):
         mass, along, cross = terms[j]
         for comp, value in enumerate((mass, cross, along)):
@@ -272,7 +275,7 @@
             moved[window, :] = moved[window, :] - metric * value
 
 
-def gather_of(traces, found, picks, block, tree):
+def gather_of(traces, found, picks, block, tree, marks):
     for face in range(FACES):
         own = range(tree * TREE_BLOCKS, (tree + 1) * TREE_BLOCKS)
         reach = range(BLOCKS) if face == 3 - tree else own
@@ -290,6 +293,7 @@
             for comp in range(4):
                 row = ((turn * BLOCKS + block) * 4 + face) * 32 + comp * 8
                 found[rows_of(row, 8), :] = total[comp]
+            marks.append(0.0 * total[3])
 
 
 def interleave(*works):
@@ -336,9 +340,10 @@
             codes[turn, four, :] = jnp.where(far, lane + LANES, lane)
         rows_kind[four, :] = kind
         rows_factor[four, :] = jnp.broadcast_to(level_row * float(LIFT * STEP), (4, LANES))
+        marks = []
         interleave(
-            volume_of(state, moved, speeds, base, into, spread(level_row)),
-            gather_of(traces, found, picks, block, tree),
+            gather_of(traces, found, picks, block, tree, marks),
+            volume_of(state, moved, speeds, base, into, spread(level_row), marks),
         )
 
     return work
@@ -355,7 +360,7 @@
         return total
 
     lead = AHEAD - one_of(narrow, (0, 7, 15, 19)) - one_of(x, (0, 10, 12, 14)) - one_of(z, (0, 10, 22, 26))
-    return jnp.clip((lead + 5 * core) // 5, 0, TREE_BLOCKS)
+    return jnp.clip((lead + 5 * core) // PER_BLOCK, 0, TREE_BLOCKS)
 
 
 def interior_kernel(
@@ -405,7 +410,7 @@
 
 def surface_kernel(
     moved_in, traces, found, codes, rows_kind, rows_factor, got_wa, got_nb, got_na, got_wb,
-    new_depth, new_moment, moved, came, near, changes, sems
+    new_depth, new_moment, moved, came, near_a, near_b, changes, sems
 ):
     del moved_in
     wide_even = (lax.axis_index("wide") & 1) == 0
@@ -431,7 +436,7 @@
             ),
         )
 
-    def body(group, carry):
+    def fetch(group, near, marks):
         for face in range(FACES):
             for turn in range(2):
                 for half in range(2):
@@ -445,6 +450,10 @@
                         near[pl.ds((turn * 4 + comp) * 64 + spot * 8, 8), :] = jnp.where(
                             far, there, found[rows_of(row, 8), :]
                         )
+                    marks.append(0.0 * there)
+                    yield
+
+    def settle(group, near, marks):
         eight = pl.ds(pl.multiple_of(group * 8, 8), 8)
         kind = rows_kind[eight, :]
         factor = rows_factor[eight, :]
@@ -463,6 +472,8 @@
                 one, two = weighted(FOLD_EVEN[a], even), weighted(FOLD_ODD[a], odd)
                 low_of[a] = one + two
                 high_of[7 - a] = one - two
+                if a % 2:
+                    yield
             left.append([jnp.where(coarse, low_of[n], own[n]) for n in range(8)])
             right.append(
                 [jnp.where(lower, low_of[n], jnp.where(upper, high_of[n], other[n])) for n in range(8)]
@@ -471,8 +482,12 @@
         one, two = [], []
         for node in range(8):
             above = [near[pl.ds((4 + comp) * 64 + node, 8, stride=8), :] for comp in range(4)]
-            one.append(numeric_flux([v[node] for v in left], [v[node] for v in right], quarter))
-            two.append(numeric_flux([v[node] for v in high], above, quarter))
+            sign = quarter
+            while marks:
+                sign = sign + marks.pop(0)
+            one.append(numeric_flux([v[node] for v in left], [v[node] for v in right], sign))
+            two.append(numeric_flux([v[node] for v in high], above, sign))
+            yield
         for comp in range(3):
             total = [one[b][comp] + two[7 - b][comp] for b in range(8)]
             differ = [one[b][comp] - two[7 - b][comp] for b in range(8)]
@@ -492,9 +507,19 @@
                     )
             for copy in copies(group * 2 + half):
                 copy.start()
+
+    def both(next_group, into, group, held):
+        marks = []
+        interleave(fetch(next_group, into, marks), settle(group, held, marks))
+
+    def body(step, carry):
+        both(2 * step + 1, near_b, 2 * step, near_a)
+        both(2 * step + 2, near_a, 2 * step + 1, near_b)
         return carry
 
-    lax.fori_loop(0, GROUPS, body, 0)
+    interleave(fetch(0, near_a, []))
+    lax.fori_loop(0, GROUPS // 2, body, 0)
+    interleave(settle(GROUPS - 1, near_a, []))
 
     def finish(block, carry):
         for copy in copies(block):
@@ -585,6 +610,7 @@
         scratch_shapes=[
             pltpu.VMEM((128, LANES), F32),
             pltpu.VMEM((512, LANES), F32),
+            pltpu.VMEM((512, LANES), F32),
             pltpu.VMEM((192, LANES), F32),
             pltpu.SemaphoreType.DMA((2, BLOCKS)),
         ],

time: 18.1 us -> 17.3 us (0.956)
  Pallas kernels: 10.1 us -> 8.64 us
  starting transfers between devices: 6.8 us -> 7.5 us
    ppermute x4, starting transfers between devices: 6.8 us -> 7.5 us  [swap(): return lax.ppermute(block, axis, route)]
    pallas_call x1, Pallas kernels: 4.41 us -> 3.7 us  [on_device(): pl.pallas_call(pack_kernel, out_shape=held + (message,) * 4 + tables + do...]
    pallas_call x1, Pallas kernels: 2.44 us -> 1.77 us  [on_device(): pl.pallas_call(interior_kernel, out_shape=done, in_specs=[VM] * 11, out_s...]
  transfers between devices with their start and end apart: 4 -> 4, of which waited for: 1 -> 1; matrix products, arithmetic and copies ran while one was open for 0% -> 0% of each run, Pallas kernels for 14% -> 10%
where the time goes in v4:
time: 17.3 us; the launch traced here: 17.2 us
  Pallas kernels  8.64 us (50%)
  starting transfers between devices  7.5 us (43%)
  between operations  0.68 us (4%)
  waiting for transfers between devices  0.32 us (2%)
    ppermute x4, starting transfers between devices, swap(): return lax.ppermute(block, axis, route)  7.5 us
    pallas_call x1, Pallas kernels, on_device(): pl.pallas_call(pack_kernel, out_shape=held + (message,) * 4 + tables + do...  3.7 us
    pallas_call x1, Pallas kernels, on_device(): pl.pallas_call(surface_kernel, out_shape=(jax.ShapeDtypeStruct((64, ELEMS...  3.17 us
    pallas_call x1, Pallas kernels, on_device(): pl.pallas_call(interior_kernel, out_shape=done, in_specs=[VM] * 11, out_s...  1.77 us
  transfers between devices with their start and end apart: 4, of which 1 were waited for; matrix products, arithmetic and copies ran while one was open for 0% of the time, Pallas kernels for 10%

profile of v4, /device:TPU:0, one launch (start us, length us, event | category | flops | bytes accessed | tf_op | source)
XLA Modules:
  0.0 17.2 jit_solution(7746782186147524554)
XLA Ops:
  0.6 3.7 %pack.1 = (f32[2560,128]{1,0:T(8,128)S(1)}, f32[1280,128]{1,0:T(8,128)S(1)}, f32[32,128]{1,0:T(8,128)S(1)}, f32[32,128]{1,0:T(8,128)S(1)}, f32[32,128]{1,0:T(8,1...) custom-call(f32[64,1280]{1,0:T(8,128)} %bitcast.6, ...), custom_call_target="tpu_custom_call" | custom-call | tf_op jit(solution)/shard_map/pack/pallas_call | solution.py:568
  4.3 0.1 collective-permute-start
  4.4 2.6 %collective-permute-start.1 = (f32[32,128]{1,0:T(8,128)S(1)}, f32[32,128]{1,0:T(8,128)S(1)}, u32[]{:S(2)}, u32[]{:S(2)}) collective-permute-start(f32[32,128]{1,0:T(8,128)S(1)} %get-tuple-element.41), channel_id=1, source_target_pairs={{0,3},{1,2},{2,1},{3,0},{4,7},{5,6},{6,5},{7,4},{8,11},{9,10},{10,... | collective-permute-start | bytes 49160 | tf_op jit(solution)/shard_map/ppermute | solution.py:541
  7.0 0.5 %collective-permute-start.2 = (f32[32,128]{1,0:T(8,128)S(1)}, f32[32,128]{1,0:T(8,128)S(1)}, u32[]{:S(2)}, u32[]{:S(2)}) collective-permute-start(f32[32,128]{1,0:T(8,128)S(1)} %get-tuple-element.42), channel_id=1, source_target_pairs={{0,1},{1,0},{2,3},{3,2},{4,5},{5,4},{6,7},{7,6},{8,9},{9,8},{10,11... | collective-permute-start | bytes 49160 | tf_op jit(solution)/shard_map/ppermute | solution.py:541
  7.5 4.4 %collective-permute-start.3 = (f32[32,128]{1,0:T(8,128)S(1)}, f32[32,128]{1,0:T(8,128)S(1)}, u32[]{:S(2)}, u32[]{:S(2)}) collective-permute-start(f32[32,128]{1,0:T(8,128)S(1)} %get-tuple-element.43), channel_id=1, source_target_pairs={{0,124},{4,8},{8,4},{12,16},{16,12},{20,24},{24,20},{28,32},{32,28... | collective-permute-start | bytes 49160 | tf_op jit(solution)/shard_map/ppermute | solution.py:541
  11.9 1.8 %interior.1 = (f32[1920,128]{1,0:T(8,128)S(1)}, f32[2560,128]{1,0:T(8,128)S(1)}, s32[2,40,128]{2,1,0:T(8,128)S(1)}, s32[40,128]{1,0:T(8,128)S(1)}, f32[40,128]{1,0:T(8,128)S(1)}) custom-call(f32[2560,128]{1,0:T(8,128)S(1)} %get-tuple-element.24.state, ...), custom_call_target="tpu_custom_call", output_to_operand_aliasing={{0}: (6, {}), {1}: (7, {}), {2}: (8, {}), {3}: (9, {}), {4}... | custom-call | flops 20000000 | bytes 2000000 | tf_op jit(solution)/shard_map/interior/pallas_call | solution.py:589
  13.6 0.0 collective-permute-done.got_wa
  13.6 0.0 collective-permute-done.1.got_nb
  13.7 0.0 collective-permute-done.2.got_na
  13.7 0.3 %collective-permute-done.3.got_wb = f32[32,128]{1,0:T(8,128)S(1)} collective-permute-done((f32[32,128]{1,0:T(8,128)S(1)}, f32[32,128]{1,0:T(8,128)S(1)}, u32[]{:S(2)}, u32[]{:S(2)}) %collective-permute-start.3) | collective-permute-done | bytes 16416 | tf_op jit(solution)/shard_map/ppermute | solution.py:541
  14.0 3.2 %surface.1 = (f32[64,1280]{1,0:T(8,128)}, f32[128,1280]{1,0:T(8,128)}, f32[1920,128]{1,0:T(8,128)S(1)}) custom-call(f32[1920,128]{1,0:T(8,128)S(1)} %get-tuple-element.35.moved_in, f32[1280,128]{1,0:T(8,128)S(1)} %get-tuple-element.25.traces, f32[2560,128]{1,0:T(8,128)S(1)} %get-tuple-element.36.found, ...), custom_call_target="tpu_custom_call", output_to_operand_aliasing={{2}: (0, {})} | custom-call | tf_op jit(solution)/shard_map/surface/pallas_call | solution.py:600
Async XLA Ops:
  4.3 9.3 %collective-permute-start = (f32[32,128]{1,0:T(8,128)S(1)}, f32[32,128]{1,0:T(8,128)S(1)}, u32[]{:S(2)}, u32[]{:S(2)}) collective-permute-start(f32[32,128]{1,0:T(8,128)S(1)} %get-tuple-element.40), channel_id=1, source_target_pairs={{0,4},{4,0},{8,12},{12,8},{16,20},{20,16},{24,28},{28,24},{32,36},... | collective-permute-start | bytes 49160 | tf_op jit(solution)/shard_map/ppermute | solution.py:541
  4.4 9.2 %collective-permute-start.1 = (f32[32,128]{1,0:T(8,128)S(1)}, f32[32,128]{1,0:T(8,128)S(1)}, u32[]{:S(2)}, u32[]{:S(2)}) collective-permute-start(f32[32,128]{1,0:T(8,128)S(1)} %get-tuple-element.41), channel_id=1, source_target_pairs={{0,3},{1,2},{2,1},{3,0},{4,7},{5,6},{6,5},{7,4},{8,11},{9,10},{10,... | collective-permute-start | bytes 49160 | tf_op jit(solution)/shard_map/ppermute | solution.py:541
  7.0 6.7 %collective-permute-start.2 = (f32[32,128]{1,0:T(8,128)S(1)}, f32[32,128]{1,0:T(8,128)S(1)}, u32[]{:S(2)}, u32[]{:S(2)}) collective-permute-start(f32[32,128]{1,0:T(8,128)S(1)} %get-tuple-element.42), channel_id=1, source_target_pairs={{0,1},{1,0},{2,3},{3,2},{4,5},{5,4},{6,7},{7,6},{8,9},{9,8},{10,11... | collective-permute-start | bytes 49160 | tf_op jit(solution)/shard_map/ppermute | solution.py:541
  7.5 6.5 %collective-permute-start.3 = (f32[32,128]{1,0:T(8,128)S(1)}, f32[32,128]{1,0:T(8,128)S(1)}, u32[]{:S(2)}, u32[]{:S(2)}) collective-permute-start(f32[32,128]{1,0:T(8,128)S(1)} %get-tuple-element.43), channel_id=1, source_target_pairs={{0,124},{4,8},{8,4},{12,16},{16,12},{20,24},{24,20},{28,32},{32,28... | collective-permute-start | bytes 49160 | tf_op jit(solution)/shard_map/ppermute | solution.py:541

commit v5 on v4

--- a/solution.py
+++ b/solution.py
@@ -11,6 +11,7 @@
 LANES = 128
 AHEAD = 35
 PER_BLOCK = 5
+FIRST_MORE = 1
 BLOCKS = ELEMS // LANES
 TREE_BLOCKS = BLOCKS // 2
 GROUPS = BLOCKS // 2
@@ -89,6 +90,10 @@
     if face == 2:
         return pl.ds(base, 8, stride=8)
     return pl.ds(base + 7, 8, stride=8)
+
+
+def trace_row(block, face, comp):
+    return (block // 2) * 256 + comp * 64 + ((block % 2) * 4 + face) * 8
 
 
 def component(face, place):
@@ -171,14 +176,17 @@
             copy.wait()
         for face in range(FACES):
             for comp in range(4):
-                traces[pl.ds(block * TRACE + (face * 4 + comp) * 8, 8), :] = state[
-                    face_rows(block * STATE + component(face, comp) * 64, face), :
-                ]
+                piece = state[face_rows(block * STATE + component(face, comp) * 64, face), :]
+                if comp == 0:
+                    height = piece
+                elif comp == 3:
+                    piece = piece + height
+                traces[pl.ds(trace_row(block, face, comp), 8), :] = piece
     for way in range(4):
         for block in range(BLOCKS):
             here = place[way] == block
             for comp in range(4):
-                got = pick(traces[pl.ds(block * TRACE + (way * 4 + comp) * 8, 8), :], lane[way])
+                got = pick(traces[pl.ds(trace_row(block, way, comp), 8), :], lane[way])
                 out[way][comp] = got if block == 0 else jnp.where(here, got, out[way][comp])
     wide_even = (lax.axis_index("wide") & 1) == 0
     narrow_even = (lax.axis_index("narrow") & 1) == 0
@@ -192,11 +200,7 @@
         copy.wait()
     work = block_worker(state, traces, kinds, trace_src, mortar_src, levels, out_refs, scratch)
 
-    def first_tree(block, carry):
-        work(block, 0)
-        return carry
-
-    lax.fori_loop(0, blocks_ahead(), first_tree, 0)
+    work_through(work, 0, blocks_ahead())
 
 
 def line_terms(height, normal, tangent, bed, marks):
@@ -286,8 +290,7 @@
             for other in reach:
                 here = place == other
                 for comp in range(4):
-                    row = other * TRACE + ((face ^ 1) * 4 + comp) * 8
-                    got = pick(traces[pl.ds(row, 8), :], lane)
+                    got = pick(traces[pl.ds(trace_row(other, face ^ 1, comp), 8), :], lane)
                     total[comp] = got if total[comp] is None else jnp.where(here, got, total[comp])
                 yield
             for comp in range(4):
@@ -339,7 +342,7 @@
             picks[pl.ds(turn * 8 + 4, 4), :] = jnp.where(far, BLOCKS, index >> 7)
             codes[turn, four, :] = jnp.where(far, lane + LANES, lane)
         rows_kind[four, :] = kind
-        rows_factor[four, :] = jnp.broadcast_to(level_row * float(LIFT * STEP), (4, LANES))
+        rows_factor[four, :] = jnp.broadcast_to(level_row * float(0.5 * LIFT * STEP), (4, LANES))
         marks = []
         interleave(
             gather_of(traces, found, picks, block, tree, marks),
@@ -349,6 +352,17 @@
     return work
 
 
+def work_through(work, start, stop):
+    for tree in range(2):
+
+        def step(block, carry, tree=tree):
+            work(block, tree)
+            return carry
+
+        low, high = tree * TREE_BLOCKS, (tree + 1) * TREE_BLOCKS
+        lax.fori_loop(jnp.maximum(start, low), jnp.minimum(stop, high), step, 0)
+
+
 def blocks_ahead():
     wide, narrow = lax.axis_index("wide"), lax.axis_index("narrow")
     x, z, core = wide >> 3, (wide >> 1) & 3, wide & 1
@@ -359,8 +373,9 @@
             total = jnp.where(at == i, jnp.int32(values[i]), total)
         return total
 
-    lead = AHEAD - one_of(narrow, (0, 7, 15, 19)) - one_of(x, (0, 10, 12, 14)) - one_of(z, (0, 10, 22, 26))
-    return jnp.clip((lead + 5 * core) // PER_BLOCK, 0, TREE_BLOCKS)
+    lead = AHEAD - one_of(narrow, (0, 0, 28, 35)) - one_of(x, (0, 10, 12, 14)) - one_of(z, (0, 10, 22, 26))
+    ahead = jnp.clip((lead + 5 * core) // PER_BLOCK, 0, TREE_BLOCKS)
+    return ahead + jnp.where((wide == 0) & (narrow < 2), FIRST_MORE, 0)
 
 
 def interior_kernel(
@@ -369,35 +384,35 @@
     out, scratch = rest[5:10], rest[10:]
     work = block_worker(state, traces, kinds, trace_src, mortar_src, levels, out, scratch)
 
-    def first_tree(block, carry):
-        work(block, 0)
-        return carry
-
-    def second_tree(block, carry):
-        work(block, 1)
-        return carry
-
-    lax.fori_loop(blocks_ahead(), TREE_BLOCKS, first_tree, 0)
-    lax.fori_loop(TREE_BLOCKS, BLOCKS, second_tree, 0)
-
-
-def numeric_flux(left, right, quarter):
+    work_through(work, blocks_ahead(), BLOCKS)
+
+
+def numeric_flux(left, right, sign):
     inv_l, inv_r = 1.0 / left[0], 1.0 / right[0]
     un_l, un_r = left[1] * inv_l, right[1] * inv_r
     un = un_l + un_r
     ut = left[2] * inv_l + right[2] * inv_r
-    half = 0.5 * jnp.maximum(
+    speed = jnp.maximum(
         jnp.abs(un_l) + left[0] * lax.rsqrt(left[0]), jnp.abs(un_r) + right[0] * lax.rsqrt(right[0])
     )
-    first = (quarter * (left[0] + right[0])) * un
+    first = (sign * (left[0] + right[0])) * un
     middle = 0.5 * first
-    second = middle * un + quarter * (left[0] * left[0] + right[0] * right[0])
+    second = middle * un + sign * (left[0] * left[0] + right[0] * right[0])
     third = middle * ut
     return (
-        first - half * ((right[0] + right[3]) - (left[0] + left[3])),
-        second - half * (right[1] - left[1]),
-        third - half * (right[2] - left[2]),
+        first - speed * (right[3] - left[3]),
+        second - speed * (right[1] - left[1]),
+        third - speed * (right[2] - left[2]),
     )
+
+
+def weighted(coefficients, values):
+    total = None
+    for coefficient, value in zip(coefficients, values):
+        if abs(coefficient) > 1e-12:
+            term = float(coefficient) * value
+            total = term if total is None else total + term
+    return total
 
 
 def weighted(coefficients, values):
@@ -424,7 +439,7 @@
         came[pl.ds(64 + comp * 8, 8), :] = jnp.where(narrow_even, narrow[1], narrow[0])
         came[pl.ds(96 + comp * 8, 8), :] = jnp.where(narrow_even, narrow[0], narrow[1])
     row_id = lax.broadcasted_iota(I32, (8, LANES), 0)
-    quarter = jnp.where((row_id & 1) == 1, 0.25, -0.25).astype(F32)
+    normal_half = jnp.where((row_id & 1) == 1, 0.5, -0.5).astype(F32)
 
     def copies(block):
         lanes = lanes_of(block)
@@ -461,7 +476,7 @@
         left, right, high = [], [], []
         for comp in range(4):
             own = [
-                traces[pl.ds(group * 256 + comp * 8 + node, 8, stride=32), :] for node in range(8)
+                traces[pl.ds(group * 256 + comp * 64 + node, 8, stride=8), :] for node in range(8)
             ]
             other = [near[pl.ds(comp * 64 + node, 8, stride=8), :] for node in range(8)]
             blend = [jnp.where(coarse, own[n], other[n]) for n in range(8)]
@@ -470,8 +485,12 @@
             low_of, high_of = [None] * 8, [None] * 8
             for a in range(8):
                 one, two = weighted(FOLD_EVEN[a], even), weighted(FOLD_ODD[a], odd)
-                low_of[a] = one + two
-                high_of[7 - a] = one - two
+                if a == 0:
+                    low_of[0], high_of[7] = blend[0], blend[7]
+                elif two is None:
+                    low_of[a] = high_of[7 - a] = one
+                else:
+                    low_of[a], high_of[7 - a] = one + two, one - two
                 if a % 2:
                     yield
             left.append([jnp.where(coarse, low_of[n], own[n]) for n in range(8)])
@@ -482,7 +501,7 @@
         one, two = [], []
         for node in range(8):
             above = [near[pl.ds((4 + comp) * 64 + node, 8, stride=8), :] for comp in range(4)]
-            sign = quarter
+            sign = normal_half
             while marks:
                 sign = sign + marks.pop(0)
             one.append(numeric_flux([v[node] for v in left], [v[node] for v in right], sign))

time: 17.3 us -> 16.4 us (0.948)
  starting transfers between devices: 7.5 us -> 7.15 us
  Pallas kernels: 8.64 us -> 8.3 us
  waiting for transfers between devices: 0.32 us -> 0.01 us
    pallas_call x1, Pallas kernels: 3.7 us -> 4.06 us  [on_device(): pl.pallas_call(pack_kernel, out_shape=held + (message,) * 4 + tables + do...]
    pallas_call x1, Pallas kernels: 3.17 us -> 2.82 us  [on_device(): pl.pallas_call(surface_kernel, out_shape=(jax.ShapeDtypeStruct((64, ELEMS...]
    ppermute x4, starting transfers between devices: 7.5 us -> 7.15 us  [swap(): return lax.ppermute(block, axis, route)]
    pallas_call x1, Pallas kernels: 1.77 us -> 1.42 us  [on_device(): pl.pallas_call(interior_kernel, out_shape=done, in_specs=[VM] * 11, out_s...]
    ppermute x4, waiting for transfers between devices: 0.32 us -> 0.01 us  [swap(): return lax.ppermute(block, axis, route)]
  transfers between devices with their start and end apart: 4 -> 4, of which waited for: 1 -> 0; matrix products, arithmetic and copies ran while one was open for 0% -> 0% of each run, Pallas kernels for 10% -> 9%
where the time goes in v5:
time: 16.4 us; the launch traced here: 16.2 us
  Pallas kernels  8.3 us (51%)
  starting transfers between devices  7.15 us (44%)
  between operations  0.69 us (4%)
    ppermute x4, starting transfers between devices, swap(): return lax.ppermute(block, axis, route)  7.15 us
    pallas_call x1, Pallas kernels, on_device(): pl.pallas_call(pack_kernel, out_shape=held + (message,) * 4 + tables + do...  4.06 us
    pallas_call x1, Pallas kernels, on_device(): pl.pallas_call(surface_kernel, out_shape=(jax.ShapeDtypeStruct((64, ELEMS...  2.82 us
    pallas_call x1, Pallas kernels, on_device(): pl.pallas_call(interior_kernel, out_shape=done, in_specs=[VM] * 11, out_s...  1.42 us
  transfers between devices with their start and end apart: 4, of which 0 were waited for; matrix products, arithmetic and copies ran while one was open for 0% of the time, Pallas kernels for 9%

profile of v5, /device:TPU:0, one launch (start us, length us, event | category | flops | bytes accessed | tf_op | source)
XLA Modules:
  0.0 16.2 jit_solution(11725491353707795712)
XLA Ops:
  0.6 4.1 %pack.1 = (f32[2560,128]{1,0:T(8,128)S(1)}, f32[1280,128]{1,0:T(8,128)S(1)}, f32[32,128]{1,0:T(8,128)S(1)}, f32[32,128]{1,0:T(8,128)S(1)}, f32[32,128]{1,0:T(8,1...) custom-call(f32[64,1280]{1,0:T(8,128)} %bitcast.6, ...), custom_call_target="tpu_custom_call" | custom-call | tf_op jit(solution)/shard_map/pack/pallas_call | solution.py:587
  4.7 0.1 collective-permute-start
  4.8 1.2 %collective-permute-start.1 = (f32[32,128]{1,0:T(8,128)S(1)}, f32[32,128]{1,0:T(8,128)S(1)}, u32[]{:S(2)}, u32[]{:S(2)}) collective-permute-start(f32[32,128]{1,0:T(8,128)S(1)} %get-tuple-element.41), channel_id=1, source_target_pairs={{0,3},{1,2},{2,1},{3,0},{4,7},{5,6},{6,5},{7,4},{8,11},{9,10},{10,... | collective-permute-start | bytes 49160 | tf_op jit(solution)/shard_map/ppermute | solution.py:560
  6.0 0.7 %collective-permute-start.2 = (f32[32,128]{1,0:T(8,128)S(1)}, f32[32,128]{1,0:T(8,128)S(1)}, u32[]{:S(2)}, u32[]{:S(2)}) collective-permute-start(f32[32,128]{1,0:T(8,128)S(1)} %get-tuple-element.42), channel_id=1, source_target_pairs={{0,1},{1,0},{2,3},{3,2},{4,5},{5,4},{6,7},{7,6},{8,9},{9,8},{10,11... | collective-permute-start | bytes 49160 | tf_op jit(solution)/shard_map/ppermute | solution.py:560
  6.6 5.2 %collective-permute-start.3 = (f32[32,128]{1,0:T(8,128)S(1)}, f32[32,128]{1,0:T(8,128)S(1)}, u32[]{:S(2)}, u32[]{:S(2)}) collective-permute-start(f32[32,128]{1,0:T(8,128)S(1)} %get-tuple-element.43), channel_id=1, source_target_pairs={{0,124},{4,8},{8,4},{12,16},{16,12},{20,24},{24,20},{28,32},{32,28... | collective-permute-start | bytes 49160 | tf_op jit(solution)/shard_map/ppermute | solution.py:560
  11.9 1.4 %interior.1 = (f32[1920,128]{1,0:T(8,128)S(1)}, f32[2560,128]{1,0:T(8,128)S(1)}, s32[2,40,128]{2,1,0:T(8,128)S(1)}, s32[40,128]{1,0:T(8,128)S(1)}, f32[40,128]{1,0:T(8,128)S(1)}) custom-call(f32[2560,128]{1,0:T(8,128)S(1)} %get-tuple-element.24.state, ...), custom_call_target="tpu_custom_call", output_to_operand_aliasing={{0}: (6, {}), {1}: (7, {}), {2}: (8, {}), {3}: (9, {}), {4}... | custom-call | flops 20000000 | bytes 2000000 | tf_op jit(solution)/shard_map/interior/pallas_call | solution.py:608
  13.3 0.0 collective-permute-done.got_wa
  13.3 0.0 collective-permute-done.1.got_nb
  13.3 0.0 collective-permute-done.2.got_na
  13.3 0.0 collective-permute-done.3.got_wb
  13.3 2.8 %surface.1 = (f32[64,1280]{1,0:T(8,128)}, f32[128,1280]{1,0:T(8,128)}, f32[1920,128]{1,0:T(8,128)S(1)}) custom-call(f32[1920,128]{1,0:T(8,128)S(1)} %get-tuple-element.35.moved_in, f32[1280,128]{1,0:T(8,128)S(1)} %get-tuple-element.25.traces, f32[2560,128]{1,0:T(8,128)S(1)} %get-tuple-element.36.found, ...), custom_call_target="tpu_custom_call", output_to_operand_aliasing={{2}: (0, {})} | custom-call | tf_op jit(solution)/shard_map/surface/pallas_call | solution.py:619
Async XLA Ops:
  4.7 8.6 %collective-permute-start = (f32[32,128]{1,0:T(8,128)S(1)}, f32[32,128]{1,0:T(8,128)S(1)}, u32[]{:S(2)}, u32[]{:S(2)}) collective-permute-start(f32[32,128]{1,0:T(8,128)S(1)} %get-tuple-element.40), channel_id=1, source_target_pairs={{0,4},{4,0},{8,12},{12,8},{16,20},{20,16},{24,28},{28,24},{32,36},... | collective-permute-start | bytes 49160 | tf_op jit(solution)/shard_map/ppermute | solution.py:560
  4.8 8.5 %collective-permute-start.1 = (f32[32,128]{1,0:T(8,128)S(1)}, f32[32,128]{1,0:T(8,128)S(1)}, u32[]{:S(2)}, u32[]{:S(2)}) collective-permute-start(f32[32,128]{1,0:T(8,128)S(1)} %get-tuple-element.41), channel_id=1, source_target_pairs={{0,3},{1,2},{2,1},{3,0},{4,7},{5,6},{6,5},{7,4},{8,11},{9,10},{10,... | collective-permute-start | bytes 49160 | tf_op jit(solution)/shard_map/ppermute | solution.py:560
  6.0 7.4 %collective-permute-start.2 = (f32[32,128]{1,0:T(8,128)S(1)}, f32[32,128]{1,0:T(8,128)S(1)}, u32[]{:S(2)}, u32[]{:S(2)}) collective-permute-start(f32[32,128]{1,0:T(8,128)S(1)} %get-tuple-element.42), channel_id=1, source_target_pairs={{0,1},{1,0},{2,3},{3,2},{4,5},{5,4},{6,7},{7,6},{8,9},{9,8},{10,11... | collective-permute-start | bytes 49160 | tf_op jit(solution)/shard_map/ppermute | solution.py:560
  6.6 6.7 %collective-permute-start.3 = (f32[32,128]{1,0:T(8,128)S(1)}, f32[32,128]{1,0:T(8,128)S(1)}, u32[]{:S(2)}, u32[]{:S(2)}) collective-permute-start(f32[32,128]{1,0:T(8,128)S(1)} %get-tuple-element.43), channel_id=1, source_target_pairs={{0,124},{4,8},{8,4},{12,16},{16,12},{20,24},{24,20},{28,32},{32,28... | collective-permute-start | bytes 49160 | tf_op jit(solution)/shard_map/ppermute | solution.py:560

commit v6 on v5

--- a/solution.py
+++ b/solution.py
@@ -502,7 +502,7 @@
         for node in range(8):
             above = [near[pl.ds((4 + comp) * 64 + node, 8, stride=8), :] for comp in range(4)]
             sign = normal_half
-            while marks:
+            for _ in range(min(2, len(marks))):
                 sign = sign + marks.pop(0)
             one.append(numeric_flux([v[node] for v in left], [v[node] for v in right], sign))
             two.append(numeric_flux([v[node] for v in high], above, sign))

time: 16.4 us -> 16.2 us (0.988)
  Pallas kernels: 8.3 us -> 8.12 us
    pallas_call x1, Pallas kernels: 2.82 us -> 2.63 us  [on_device(): pl.pallas_call(surface_kernel, out_shape=(jax.ShapeDtypeStruct((64, ELEMS...]
where the time goes in v6:
time: 16.2 us; the launch traced here: 16 us
  Pallas kernels  8.12 us (50%)
  starting transfers between devices  7.15 us (44%)
  between operations  0.69 us (4%)
    ppermute x4, starting transfers between devices, swap(): return lax.ppermute(block, axis, route)  7.15 us
    pallas_call x1, Pallas kernels, on_device(): pl.pallas_call(pack_kernel, out_shape=held + (message,) * 4 + tables + do...  4.06 us
    pallas_call x1, Pallas kernels, on_device(): pl.pallas_call(surface_kernel, out_shape=(jax.ShapeDtypeStruct((64, ELEMS...  2.63 us
    pallas_call x1, Pallas kernels, on_device(): pl.pallas_call(interior_kernel, out_shape=done, in_specs=[VM] * 11, out_s...  1.42 us
  transfers between devices with their start and end apart: 4, of which 0 were waited for; matrix products, arithmetic and copies ran while one was open for 0% of the time, Pallas kernels for 9%

profile of v6, /device:TPU:0, one launch (start us, length us, event | category | flops | bytes accessed | tf_op | source)
XLA Modules:
  0.0 16.0 jit_solution(4573125837659747407)
XLA Ops:
  0.6 4.1 %pack.1 = (f32[2560,128]{1,0:T(8,128)S(1)}, f32[1280,128]{1,0:T(8,128)S(1)}, f32[32,128]{1,0:T(8,128)S(1)}, f32[32,128]{1,0:T(8,128)S(1)}, f32[32,128]{1,0:T(8,1...) custom-call(f32[64,1280]{1,0:T(8,128)} %bitcast.6, ...), custom_call_target="tpu_custom_call" | custom-call | tf_op jit(solution)/shard_map/pack/pallas_call | solution.py:587
  4.7 0.1 collective-permute-start
  4.8 1.2 %collective-permute-start.1 = (f32[32,128]{1,0:T(8,128)S(1)}, f32[32,128]{1,0:T(8,128)S(1)}, u32[]{:S(2)}, u32[]{:S(2)}) collective-permute-start(f32[32,128]{1,0:T(8,128)S(1)} %get-tuple-element.41), channel_id=1, source_target_pairs={{0,3},{1,2},{2,1},{3,0},{4,7},{5,6},{6,5},{7,4},{8,11},{9,10},{10,... | collective-permute-start | bytes 49160 | tf_op jit(solution)/shard_map/ppermute | solution.py:560
  6.0 0.7 %collective-permute-start.2 = (f32[32,128]{1,0:T(8,128)S(1)}, f32[32,128]{1,0:T(8,128)S(1)}, u32[]{:S(2)}, u32[]{:S(2)}) collective-permute-start(f32[32,128]{1,0:T(8,128)S(1)} %get-tuple-element.42), channel_id=1, source_target_pairs={{0,1},{1,0},{2,3},{3,2},{4,5},{5,4},{6,7},{7,6},{8,9},{9,8},{10,11... | collective-permute-start | bytes 49160 | tf_op jit(solution)/shard_map/ppermute | solution.py:560
  6.6 5.2 %collective-permute-start.3 = (f32[32,128]{1,0:T(8,128)S(1)}, f32[32,128]{1,0:T(8,128)S(1)}, u32[]{:S(2)}, u32[]{:S(2)}) collective-permute-start(f32[32,128]{1,0:T(8,128)S(1)} %get-tuple-element.43), channel_id=1, source_target_pairs={{0,124},{4,8},{8,4},{12,16},{16,12},{20,24},{24,20},{28,32},{32,28... | collective-permute-start | bytes 49160 | tf_op jit(solution)/shard_map/ppermute | solution.py:560
  11.9 1.4 %interior.1 = (f32[1920,128]{1,0:T(8,128)S(1)}, f32[2560,128]{1,0:T(8,128)S(1)}, s32[2,40,128]{2,1,0:T(8,128)S(1)}, s32[40,128]{1,0:T(8,128)S(1)}, f32[40,128]{1,0:T(8,128)S(1)}) custom-call(f32[2560,128]{1,0:T(8,128)S(1)} %get-tuple-element.24.state, ...), custom_call_target="tpu_custom_call", output_to_operand_aliasing={{0}: (6, {}), {1}: (7, {}), {2}: (8, {}), {3}: (9, {}), {4}... | custom-call | flops 20000000 | bytes 2000000 | tf_op jit(solution)/shard_map/interior/pallas_call | solution.py:608
  13.3 0.0 collective-permute-done.got_wa
  13.3 0.0 collective-permute-done.1.got_nb
  13.3 0.0 collective-permute-done.2.got_na
  13.3 0.0 collective-permute-done.3.got_wb
  13.3 2.6 %surface.1 = (f32[64,1280]{1,0:T(8,128)}, f32[128,1280]{1,0:T(8,128)}, f32[1920,128]{1,0:T(8,128)S(1)}) custom-call(f32[1920,128]{1,0:T(8,128)S(1)} %get-tuple-element.35.moved_in, f32[1280,128]{1,0:T(8,128)S(1)} %get-tuple-element.25.traces, f32[2560,128]{1,0:T(8,128)S(1)} %get-tuple-element.36.found, ...), custom_call_target="tpu_custom_call", output_to_operand_aliasing={{2}: (0, {})} | custom-call | tf_op jit(solution)/shard_map/surface/pallas_call | solution.py:619
Async XLA Ops:
  4.7 8.6 %collective-permute-start = (f32[32,128]{1,0:T(8,128)S(1)}, f32[32,128]{1,0:T(8,128)S(1)}, u32[]{:S(2)}, u32[]{:S(2)}) collective-permute-start(f32[32,128]{1,0:T(8,128)S(1)} %get-tuple-element.40), channel_id=1, source_target_pairs={{0,4},{4,0},{8,12},{12,8},{16,20},{20,16},{24,28},{28,24},{32,36},... | collective-permute-start | bytes 49160 | tf_op jit(solution)/shard_map/ppermute | solution.py:560
  4.8 8.5 %collective-permute-start.1 = (f32[32,128]{1,0:T(8,128)S(1)}, f32[32,128]{1,0:T(8,128)S(1)}, u32[]{:S(2)}, u32[]{:S(2)}) collective-permute-start(f32[32,128]{1,0:T(8,128)S(1)} %get-tuple-element.41), channel_id=1, source_target_pairs={{0,3},{1,2},{2,1},{3,0},{4,7},{5,6},{6,5},{7,4},{8,11},{9,10},{10,... | collective-permute-start | bytes 49160 | tf_op jit(solution)/shard_map/ppermute | solution.py:560
  6.0 7.4 %collective-permute-start.2 = (f32[32,128]{1,0:T(8,128)S(1)}, f32[32,128]{1,0:T(8,128)S(1)}, u32[]{:S(2)}, u32[]{:S(2)}) collective-permute-start(f32[32,128]{1,0:T(8,128)S(1)} %get-tuple-element.42), channel_id=1, source_target_pairs={{0,1},{1,0},{2,3},{3,2},{4,5},{5,4},{6,7},{7,6},{8,9},{9,8},{10,11... | collective-permute-start | bytes 49160 | tf_op jit(solution)/shard_map/ppermute | solution.py:560
  6.6 6.7 %collective-permute-start.3 = (f32[32,128]{1,0:T(8,128)S(1)}, f32[32,128]{1,0:T(8,128)S(1)}, u32[]{:S(2)}, u32[]{:S(2)}) collective-permute-start(f32[32,128]{1,0:T(8,128)S(1)} %get-tuple-element.43), channel_id=1, source_target_pairs={{0,124},{4,8},{8,4},{12,16},{16,12},{20,24},{24,20},{28,32},{32,28... | collective-permute-start | bytes 49160 | tf_op jit(solution)/shard_map/ppermute | solution.py:560
